TPU v7x, 256 devices: a whole 4x4x8 slice. The times are simulated.
256 devices in a mesh: ta: 32 (over z, x_lo, core), dev: 8 (over y, x_hi).
Axes of the slice: x: 4 (x_hi: 2, x_lo: 2; x = x_hi * 2 + x_lo), y: 4, z: 8, core: 2. Of those that a mesh axis runs over, the one named last changes fastest.
Arguments:
- raw_integrals: bfloat16 [512, 64, 36864], P(('ta', 'dev')), may hold values from -6 to 6
- metric: bfloat16 [512, 64, 64], P(('ta', 'dev')), may hold values from -0.125 to 0.125
- aux_list: int32 [512, 3], P(('ta', 'dev')), may hold values from 0 to 1023, as said below
- density_list: int32 [1024, 8], replicated, may hold values from 0 to 1023, as said below
- density_blocks: bfloat16 [1024, 8, 64, 64], P('ta', 'dev'), may hold values from -0.4375 to 0.4375
Outputs:
- exchange: float32 [1024, 8, 64, 64], P('ta', 'dev')
Inputs may be any that keep to these rules, and one draw needn't show every extreme that they name: `aux_list`: row a names 3 different orbital blocks, all among blocks s to s + 4 taken modulo 1024 for some s from g * 32 - 4 to (g + 1) * 32 - 1, where g = a // 16 is the index along ta of the device holding row a. `density_list`: row r names each of the column blocks r - 3 to r + 4, taken modulo 1024, once, in some order.
All inputs are finite; a program needn't handle non-finite values.
Results may differ from a plain program's by a relative error of at most 0.0065.
Values may be sent and summed in bfloat16 or wider, within the bound.
No kernel may reach another device: no remote copies, remote signals or barrier semaphores. Data moves between devices by JAX's collectives and lax.ppermute only.
A program may use at most 192 MiB of HBM per device.

v0:
```python
import jax
import jax.numpy as jnp
from jax import lax
from jax.sharding import PartitionSpec as P


def extended(shard, sides, width):
    for axis, dim in sides:
        peers, length = (lax.axis_size(axis), shard.shape[dim])
        up = [(i, (i + 1) % peers) for i in range(peers)]
        down = [(j, i) for i, j in up]
        last = lax.slice_in_dim(shard, length - width, length, axis=dim)
        leading = lax.slice_in_dim(shard, 0, width, axis=dim)
        before = lax.ppermute(last, axis, up)
        after = lax.ppermute(leading, axis, down)
        shard = jnp.concatenate([before, shard, after], axis=dim)
    return shard


def from_behind(value, axis, steps):
    count = lax.axis_size(axis)
    pairs = [(source, (source + steps) % count) for source in range(count)]
    return lax.ppermute(value, axis, pairs)


def block_terms(integral_block, metric_block, orbital_ids, column_ids, density_rows):
    functions = integral_block.shape[0]
    orbitals = density_rows.shape[-1]
    listed = orbital_ids.shape[0]
    window = listed * orbitals
    fitted = jnp.dot(metric_block, integral_block, preferred_element_type=jnp.float32)
    fitted = fitted.astype(jnp.bfloat16).reshape(functions, window, window)
    matches = (column_ids[:, None, :] == orbital_ids[None, :, None]).astype(jnp.float32)
    window_density = jnp.einsum("ijk,ikab->iajb", matches, density_rows.astype(jnp.float32))
    window_density = window_density.astype(jnp.bfloat16).reshape(window, window)
    mixed = jnp.dot(
        fitted.reshape(functions * window, window),
        window_density,
        preferred_element_type=jnp.float32,
    )
    mixed = mixed.astype(jnp.bfloat16).reshape(functions, window, window)
    contribution = lax.dot_general(
        mixed, fitted, (((0, 2), (0, 2)), ((), ())), preferred_element_type=jnp.float32
    )
    return jnp.einsum(
        "ijk,iajb->ikab", matches, contribution.reshape(listed, orbitals, listed, orbitals)
    )


def per_device(raw_integrals, metric, aux_list, density_list, density_blocks):
    slab_rows = density_blocks.shape[0]
    block_count = slab_rows * lax.axis_size("ta")
    first_block = (lax.axis_index("ta") - 1) * slab_rows % block_count
    panel_rows = lax.all_gather(density_blocks, "dev", axis=1, tiled=True)
    near_rows = extended(panel_rows, (("ta", 0),), slab_rows)

    def one_block(totals, operands):
        integral_block, metric_block, orbital_ids = operands
        near_ids = (orbital_ids - first_block) % block_count
        pieces = block_terms(
            integral_block,
            metric_block,
            orbital_ids,
            density_list[orbital_ids],
            near_rows[near_ids],
        )
        return (totals.at[near_ids].add(pieces), None)

    start_totals = jnp.zeros((3 * slab_rows,) + near_rows.shape[1:], jnp.float32)
    totals, unused = lax.scan(one_block, start_totals, (raw_integrals, metric, aux_list))
    from_after = from_behind(totals[:slab_rows], "ta", -1)
    from_before = from_behind(totals[2 * slab_rows :], "ta", 1)
    own_rows = totals[slab_rows : 2 * slab_rows] + from_after + from_before
    return lax.psum_scatter(own_rows, "dev", scatter_dimension=1, tiled=True)


def solution(mesh):
    placed = (
        P(("ta", "dev"), None, None),
        P(("ta", "dev"), None, None),
        P(("ta", "dev"), None),
        P(),
        P("ta", "dev", None, None),
    )
    return jax.shard_map(
        per_device,
        mesh=mesh,
        in_specs=placed,
        out_specs=P("ta", "dev", None, None),
        check_vma=False,
    )
```

profile of v0, /device:TPU:8, one launch (start us, length us, event | category | flops | bytes accessed | tf_op | source)
XLA Modules:
  0.0 920.9 jit_solution(17602993969628103332)
XLA Ops:
  7.3 80.8 %all-gather.2.cloned.1.call-done = bf16[32,8,64,64]{3,2,1,0:T(8,128)(2,1)} async-done(((bf16[32,1,64,64]{3,2,1,0:T(8,128)(2,1)}), bf16[32,8,64,64]{3,2,1,0:T(8,128)(2,1)}) %all-gather.2.cloned.1.call-update) | async-done | bytes 2097168 | tf_op jit(solution)/shard_map/all_gather | solution.py:54
  88.1 3.9 collective-permute-start.1
  92.9 45.6 %collective-permute-done = bf16[32,8,64,64]{3,2,1,0:T(8,128)(2,1)} collective-permute-done((bf16[32,8,64,64]{3,2,1,0:T(8,128)(2,1)}, bf16[32,8,64,64]{3,2,1,0:T(8,128)(2,1)}, u32[]{:S(2)}, u32[]{:S(2)}) %collective-permute-start) | collective-permute-done | bytes 2097184 | tf_op jit(solution)/shard_map/ppermute | solution.py:14
  138.5 12.1 %pad_maximum_fusion = bf16[96,8,64,64]{3,2,1,0:T(8,128)(2,1)} fusion(bf16[32,8,64,64]{3,2,1,0:T(8,128)(2,1)} %collective-permute-done.1, bf16[32,8,64,64]{3,2,1,0:T(8,128)(2,1)} %all-gather.2.cloned.1.call-done, bf16[32,8,64,64]{3,2,1,0:T(8,128)(2,1)} %collective-permute-done), kind=kLoop, calls=%fused_computation.41 | loop fusion | flops 6291456 | bytes 12582912 | tf_op jit(solution)/shard_map/concatenate | solution.py:16
  150.6 11.5 %broadcast_in_dim.2 = f32[96,8,64,64]{3,2,1,0:T(8,128)} broadcast(f32[]{:T(128)} %constant.67.clone.1), dimensions={} | broadcast | bytes 12582916 | tf_op jit(solution)/shard_map/broadcast_in_dim | solution.py:69
  162.2 159.8 %while.12 = (s32[]{:T(128)}, f32[96,8,64,64]{3,2,1,0:T(8,128)}, s32[2,3]{1,0:T(2,128)S(1)}, s32[]{:T(128)}, s32[1024,8]{1,0:T(8,128)S(1)}, /*index=5*/bf16[2,64,...) while((s32[]{:T(128)}, f32[96,8,64,64]{3,2,1,0:T(8,128)}, ...), condition=%wide.region_2.3_spmd, body=%wide.region_0.2_spmd.sunk | while | flops 2119964928 | bytes 69478016 | solution.py:70
  162.8 5.2 gather_fusion
  168.5 5.9 convolution_convert_fusion.5
  174.4 10.7 %reshape.169 = bf16[12288,192]{1,0:T(8,128)(2,1)} reshape(bf16[64,36864]{1,0:T(8,128)(2,1)} %convolution_convert_fusion.5) | data formatting | bytes 9437184 | tf_op jit(solution)/shard_map/while/body/eval_jaxpr/reshape;while/body/eval_jaxpr/reshape | solution.py:37
  185.1 7.2 convolution_convert_fusion.6
  192.3 10.8 %reshape.171 = bf16[64,192,192]{1,0,2:T(8,128)(2,1)} reshape(bf16[12288,192]{0,1:T(8,128)(2,1)} %convolution_convert_fusion.6) | data formatting | bytes 9437184 | tf_op jit(solution)/shard_map/while/body/eval_jaxpr/reshape | solution.py:41
  203.1 11.7 %copy.58 = bf16[64,192,192]{2,0,1:T(8,128)(2,1)} copy(bf16[64,192,192]{1,0,2:T(8,128)(2,1)} %reshape.171) | data formatting | bytes 9437184 | tf_op jit(solution)/shard_map/while/body/eval_jaxpr/reshape | solution.py:41
  214.8 10.8 %reshape.168 = bf16[64,192,192]{2,1,0:T(8,128)(2,1)} reshape(bf16[64,36864]{1,0:T(8,128)(2,1)} %convolution_convert_fusion.5) | data formatting | bytes 9437184 | tf_op jit(solution)/shard_map/while/body/eval_jaxpr/reshape | solution.py:32
  225.5 13.0 %fusion.61 = bf16[3,64,3,64]{3,1,2,0:T(8,128)(2,1)S(1)} fusion(bf16[3,64,64,192]{3,1,0,2:T(8,128)(2,1)} %bitcast.80, bf16[3,64,64,192,1]{3,2,1,0,4:T(8,128)(2,1)} %bitcast.79), kind=kOutput, calls=%fused_computation.12.clone.1 | convolution fusion | flops 905969664 | bytes 9510912 | tf_op jit(solution)/shard_map/while/body/eval_jaxpr/dot_general | solution.py:42
  239.1 3.0 scatter_fusion
  242.7 5.2 gather_fusion
  248.5 5.9 convolution_convert_fusion.5
  254.3 10.7 %reshape.169 = bf16[12288,192]{1,0:T(8,128)(2,1)} reshape(bf16[64,36864]{1,0:T(8,128)(2,1)} %convolution_convert_fusion.5) | data formatting | bytes 9437184 | tf_op jit(solution)/shard_map/while/body/eval_jaxpr/reshape;while/body/eval_jaxpr/reshape | solution.py:37
  265.1 7.2 convolution_convert_fusion.6
  272.3 10.8 %reshape.171 = bf16[64,192,192]{1,0,2:T(8,128)(2,1)} reshape(bf16[12288,192]{0,1:T(8,128)(2,1)} %convolution_convert_fusion.6) | data formatting | bytes 9437184 | tf_op jit(solution)/shard_map/while/body/eval_jaxpr/reshape | solution.py:41
  283.0 11.7 %copy.58 = bf16[64,192,192]{2,0,1:T(8,128)(2,1)} copy(bf16[64,192,192]{1,0,2:T(8,128)(2,1)} %reshape.171) | data formatting | bytes 9437184 | tf_op jit(solution)/shard_map/while/body/eval_jaxpr/reshape | solution.py:41
  294.7 10.8 %reshape.168 = bf16[64,192,192]{2,1,0:T(8,128)(2,1)} reshape(bf16[64,36864]{1,0:T(8,128)(2,1)} %convolution_convert_fusion.5) | data formatting | bytes 9437184 | tf_op jit(solution)/shard_map/while/body/eval_jaxpr/reshape | solution.py:32
  305.5 13.0 %fusion.61 = bf16[3,64,3,64]{3,1,2,0:T(8,128)(2,1)S(1)} fusion(bf16[3,64,64,192]{3,1,0,2:T(8,128)(2,1)} %bitcast.80, bf16[3,64,64,192,1]{3,2,1,0,4:T(8,128)(2,1)} %bitcast.79), kind=kOutput, calls=%fused_computation.12.clone.1 | convolution fusion | flops 905969664 | bytes 9510912 | tf_op jit(solution)/shard_map/while/body/eval_jaxpr/dot_general | solution.py:42
  319.1 2.9 scatter_fusion
  322.0 9.3 %fusion.30 = (f32[32,8,64,64]{3,2,1,0:T(8,128)}, f32[32,8,64,64]{3,2,1,0:T(8,128)S(1)}) fusion(f32[96,8,64,64]{3,2,1,0:T(8,128)} %get-tuple-element.107), kind=kLoop, calls=%fused_computation.44 | loop fusion | bytes 16777216 | tf_op jit(solution)/shard_map/slice | solution.py:71
  331.3 3.7 collective-permute-start.2
  335.0 39.6 %collective-permute-start.3 = (f32[32,8,64,64]{3,2,1,0:T(8,128)S(1)}, f32[32,8,64,64]{3,2,1,0:T(8,128)}, u32[]{:S(2)}, u32[]{:S(2)}) collective-permute-start(f32[32,8,64,64]{3,2,1,0:T(8,128)S(1)} %get-tuple-element.161), channel_id=1, source_target_pairs={{0,8},{8,16},{16,24},{24,32},{32,40},{40,48},{48,56},{56,64},{64,7... | collective-permute-start | bytes 12582920 | tf_op jit(solution)/shard_map/ppermute | solution.py:23
  374.6 51.8 %collective-permute-done.2 = f32[32,8,64,64]{3,2,1,0:T(8,128)S(1)} collective-permute-done((f32[32,8,64,64]{3,2,1,0:T(8,128)}, f32[32,8,64,64]{3,2,1,0:T(8,128)S(1)}, u32[]{:S(2)}, u32[]{:S(2)}) %collective-permute-start.2) | collective-permute-done | bytes 4194336 | tf_op jit(solution)/shard_map/ppermute | solution.py:23
  426.3 42.3 %collective-permute-done.3 = f32[32,8,64,64]{3,2,1,0:T(8,128)} collective-permute-done((f32[32,8,64,64]{3,2,1,0:T(8,128)S(1)}, f32[32,8,64,64]{3,2,1,0:T(8,128)}, u32[]{:S(2)}, u32[]{:S(2)}) %collective-permute-start.3) | collective-permute-done | bytes 4194336 | tf_op jit(solution)/shard_map/ppermute | solution.py:23
  468.7 9.3 %add_add_fusion = f32[32,8,64,64]{3,2,1,0:T(8,128)} fusion(f32[32,8,64,64]{3,2,1,0:T(8,128)} %collective-permute-done.3, f32[32,8,64,64]{3,2,1,0:T(8,128)S(1)} %collective-permute-done.2, f32[96,8,64,64]{3,2,1,0:T(8,128)} %get-tuple-element.107), kind=kLoop, calls=%fused_computation.42 | loop fusion | flops 2097152 | bytes 16777216 | tf_op jit(solution)/shard_map/add | solution.py:73
  479.2 431.9 %all-reduce.3.cloned.1.call-done = f32[32,8,64,64]{3,2,1,0:T(8,128)} async-done(((f32[32,8,64,64]{3,2,1,0:T(8,128)}), f32[32,8,64,64]{3,2,1,0:T(8,128)}) %all-reduce.3.cloned.1.call-update) | async-done | bytes 4194320
  911.1 2.9 constant_dynamic-slice_fusion.1
  (30 shorter events, 6.2 us)
Async XLA Ops:
  6.5 81.5 %all-gather.2.cloned.1.call-start = ((), (), s32[]{:S(2)}) async-start(), calls=%async_computation | async-start | bytes 4718592 | tf_op jit(solution)/shard_map/all_gather | solution.py:54
  7.3 903.9 %all-reduce.3.cloned.1.call-start = ((), (), s32[]{:S(2)}) async-start(), calls=%async_computation.1 | async-start | bytes 16777216
  88.1 50.5 %collective-permute-start = (bf16[32,8,64,64]{3,2,1,0:T(8,128)(2,1)}, bf16[32,8,64,64]{3,2,1,0:T(8,128)(2,1)}, u32[]{:S(2)}, u32[]{:S(2)}) collective-permute-start(bf16[32,8,64,64]{3,2,1,0:T(8,128)(2,1)} %all-gather.2.cloned.1.call-done), channel_id=1, source_target_pairs={{0,8},{8,16},{16,24},{24,32},{32,40},{40,48},{48,56},{56,64},{64,7... | collective-permute-start | bytes 6291464 | tf_op jit(solution)/shard_map/ppermute | solution.py:14
  88.1 50.5 %collective-permute-start.1 = (bf16[32,8,64,64]{3,2,1,0:T(8,128)(2,1)}, bf16[32,8,64,64]{3,2,1,0:T(8,128)(2,1)}, u32[]{:S(2)}, u32[]{:S(2)}) collective-permute-start(bf16[32,8,64,64]{3,2,1,0:T(8,128)(2,1)} %all-gather.2.cloned.1.call-done), channel_id=1, source_target_pairs={{8,0},{16,8},{24,16},{32,24},{40,32},{48,40},{56,48},{64,56},{72,6... | collective-permute-start | bytes 6291464 | tf_op jit(solution)/shard_map/ppermute | solution.py:15
  150.6 11.5 %copy-start = (bf16[2,64,64]{2,1,0:T(8,128)(2,1)S(1)}, bf16[2,64,64]{2,1,0:T(8,128)(2,1)}, u32[]{:S(2)}) copy-start(bf16[2,64,64]{2,1,0:T(8,128)(2,1)} %param.8) | copy-start | bytes 49156
  150.6 11.5 %copy-start.1 = (s32[2,3]{1,0:T(2,128)S(1)}, s32[2,3]{1,0:T(2,128)}, u32[]{:S(2)}) copy-start(s32[2,3]{1,0:T(2,128)} %param.9) | copy-start | bytes 76
  331.3 95.1 %collective-permute-start.2 = (f32[32,8,64,64]{3,2,1,0:T(8,128)}, f32[32,8,64,64]{3,2,1,0:T(8,128)S(1)}, u32[]{:S(2)}, u32[]{:S(2)}) collective-permute-start(f32[32,8,64,64]{3,2,1,0:T(8,128)} %get-tuple-element.160), channel_id=1, source_target_pairs={{0,248},{8,0},{16,8},{24,16},{32,24},{40,32},{48,40},{56,48},{64,5... | collective-permute-start | bytes 12582920 | tf_op jit(solution)/shard_map/ppermute | solution.py:23
  335.0 133.6 %collective-permute-start.3 = (f32[32,8,64,64]{3,2,1,0:T(8,128)S(1)}, f32[32,8,64,64]{3,2,1,0:T(8,128)}, u32[]{:S(2)}, u32[]{:S(2)}) collective-permute-start(f32[32,8,64,64]{3,2,1,0:T(8,128)S(1)} %get-tuple-element.161), channel_id=1, source_target_pairs={{0,8},{8,16},{16,24},{24,32},{32,40},{40,48},{48,56},{56,64},{64,7... | collective-permute-start | bytes 12582920 | tf_op jit(solution)/shard_map/ppermute | solution.py:23
  477.9 0.7 copy-start.2
Sparse Core Ops, SparseCore 0:
  10.0 78.0 all-gather.1
  478.1 433.0 all-reduce.2
where the time goes:
time: 924 us; the launch traced here: 921 us
  waiting for transfers between devices  653 us (71%)
  local copies, waits for them, and re-layouts  126 us (14%)
  matrix products  53.7 us (6%)
  starting transfers between devices  47.2 us (5%)
  other arithmetic  27.4 us (3%)
  between operations  13.4 us (1%)
    unnamed x3, waiting for transfers between devices  433 us
    ppermute x2, waiting for transfers between devices, from_behind(): return lax.ppermute(value, axis, pairs)  94.1 us
    all_gather x1, waiting for transfers between devices, per_device(): panel_rows = lax.all_gather(density_blocks, 'dev', axis=1, tiled=True)  80.8 us
    ppermute x1, waiting for transfers between devices, extended(): before = lax.ppermute(last, axis, up)  45.6 us
    reshape x4, local copies, waits for them, and re-layouts, block_terms(): mixed = mixed.astype(jnp.bfloat16).reshape(functions, window, window)  44.9 us
    ppermute x2, starting transfers between devices, from_behind(): return lax.ppermute(value, axis, pairs)  43.3 us
    dot_general x2, matrix products, block_terms(): lax.dot_general(mixed, fitted, (((0, 2), (0, 2)), ((), ())), preferred_el...  26.1 us
    reshape x2, local copies, waits for them, and re-layouts, block_terms(): fitted = fitted.astype(jnp.bfloat16).reshape(functions, window, window)  21.5 us
  transfers between devices with their start and end apart: 6, of which 5 were waited for; matrix products, arithmetic and copies ran while one was open for 0% of the time, Pallas kernels for 0%

commit v1 on v0

v1 whole, which is shorter than its diff:
```python
import functools

import jax
import jax.numpy as jnp
from jax import lax
from jax.experimental import pallas as pl
from jax.experimental.pallas import tpu as pltpu
from jax.sharding import PartitionSpec as P

BF16 = jnp.bfloat16
F32 = jnp.float32
HALO = 4
VMEM_LIMIT = 50 * 2**20


def whole(shape):
    return pl.BlockSpec(shape, lambda *_: (0,) * len(shape))


def fit_kernel(rows, stride, window, metric_ref, raw_ref, *refs):
    out_ref, low, high = refs[-3:]
    aux = metric_ref.shape[1]
    metric = metric_ref[0]
    for pair in range(rows // 2):
        lanes = pl.ds(pair * 2 * window, 2 * window)
        both = jnp.dot(metric, raw_ref[0, :, lanes], preferred_element_type=F32)
        turned = pltpu.roll(both, window, axis=1)
        for half, values in enumerate((both, turned)):
            at = pl.ds(2 * pair + half, aux, stride=stride)
            low[at, :] = values[:, :128]
            high[at, :] = values[:, 128:256]
    out_ref[0, :, :, :128] = low[...].reshape(aux, stride, 128)[:, :rows].astype(BF16)
    rest = window - 128
    upper = high[:, :rest].reshape(aux, stride, rest)[:, :rows]
    out_ref[0, :, :, 128:] = upper.astype(BF16)


def fit(raw, metric, window, which, onto=None, rows=96):
    count, aux, merged = raw.shape
    stride = rows + 8
    operands = [metric, raw]
    in_specs = [
        pl.BlockSpec((1, aux, aux), lambda c: (which, 0, 0)),
        pl.BlockSpec((1, aux, rows * window), lambda c: (which, 0, c)),
    ]
    if onto is not None:
        operands.append(onto)
        in_specs.append(pl.BlockSpec(memory_space=pl.ANY))
    return pl.pallas_call(
        functools.partial(fit_kernel, rows, stride, window),
        grid=(window // rows,),
        in_specs=in_specs,
        out_specs=pl.BlockSpec((1, aux, rows, window), lambda c: (which, 0, c, 0)),
        out_shape=jax.ShapeDtypeStruct((count, aux, window, window), BF16),
        scratch_shapes=[pltpu.VMEM((aux * stride, 128), F32)] * 2,
        input_output_aliases={} if onto is None else {2: 0},
        compiler_params=pltpu.CompilerParams(vmem_limit_bytes=VMEM_LIMIT),
        cost_estimate=pl.CostEstimate(
            flops=2 * aux * aux * merged, bytes_accessed=5 * aux * merged, transcendentals=0
        ),
        name="fit",
    )(*operands)


def pack_kernel(rows, own_ref, before_ref, after_ref, out_ref, near):
    slab = own_ref.shape[0]
    near[:HALO] = before_ref[...]
    near[HALO : HALO + slab] = own_ref[...]
    near[HALO + slab :] = after_ref[...]
    peers, listed = out_ref.shape[:2]
    for peer in range(peers):
        for i in range(listed):
            at = peer * 2 * listed + i
            pair = (near[rows[at]], near[rows[at + listed]])
            out_ref[peer, i] = jnp.concatenate(pair, axis=1)


def pack(rows, own, before, after, peers, listed):
    slab, orbitals = own.shape[:2]
    shape = (peers, listed, orbitals, 2 * orbitals)
    return pl.pallas_call(
        pack_kernel,
        grid_spec=pltpu.PrefetchScalarGridSpec(
            num_scalar_prefetch=1,
            grid=(1,),
            in_specs=[whole(own.shape), whole(before.shape), whole(after.shape)],
            out_specs=whole(shape),
            scratch_shapes=[pltpu.VMEM((slab + 2 * HALO, orbitals, orbitals), BF16)],
        ),
        out_shape=jax.ShapeDtypeStruct(shape, BF16),
        cost_estimate=pl.CostEstimate(flops=0, bytes_accessed=2**20, transcendentals=0),
        name="pack",
    )(rows, own, before, after)


def mix_kernel(part, steps, slots, fit_ref, recv_ref, out_ref, dens, acc):
    a, t = pl.program_id(0), pl.program_id(1)
    listed, ob = recv_ref.shape[1:3]
    window = listed * ob

    @pl.when((a == 0) & (t == 0))
    def _():
        out_ref[...] = jnp.zeros_like(out_ref)

    @pl.when(t == 0)
    def _():
        for i in range(listed):
            blocks = []
            for j in range(listed):
                slot = slots[(a * listed + i) * listed + j]
                pair = recv_ref[jnp.maximum(slot, 0), i].astype(F32)
                block = jnp.where(a == 0, pair[:, :ob], pair[:, ob:])
                blocks.append(jnp.where(slot >= 0, block, 0.0))
            dens[i * ob : (i + 1) * ob, :] = jnp.concatenate(blocks, axis=1).astype(BF16)
        acc[...] = jnp.zeros_like(acc)

    fitted = fit_ref[0].reshape(part * window, window)
    mixed = jnp.dot(fitted, dens[...], preferred_element_type=F32).astype(BF16)
    total = None
    for q in range(part):
        term = lax.dot_general(
            mixed[q * window : (q + 1) * window],
            fit_ref[0, q],
            (((1,), (1,)), ((), ())),
            preferred_element_type=F32,
        )
        total = term if total is None else total + term
    acc[...] += total

    for half in range(2):

        @pl.when((t == steps - 1) & (a == half))
        def _():
            for i in range(listed):
                for j in range(listed):
                    slot = slots[(half * listed + i) * listed + j]
                    block = acc[i * ob : (i + 1) * ob, j * ob : (j + 1) * ob]

                    @pl.when(slot >= 0)
                    def _():
                        out_ref[slot, i, :, half * ob : (half + 1) * ob] = block.astype(BF16)


def mix(slots, fitted, received, part=32):
    count, aux, window, _ = fitted.shape
    shape = received.shape
    return pl.pallas_call(
        functools.partial(mix_kernel, part, aux // part),
        grid_spec=pltpu.PrefetchScalarGridSpec(
            num_scalar_prefetch=1,
            grid=(count, aux // part),
            in_specs=[
                pl.BlockSpec((1, part, window, window), lambda a, t, s: (a, t, 0, 0)),
                whole(shape),
            ],
            out_specs=whole(shape),
            scratch_shapes=[pltpu.VMEM((window, window), BF16), pltpu.VMEM((window, window), F32)],
        ),
        out_shape=jax.ShapeDtypeStruct(shape, BF16),
        compiler_params=pltpu.CompilerParams(vmem_limit_bytes=VMEM_LIMIT),
        cost_estimate=pl.CostEstimate(
            flops=4 * count * aux * window**3,
            bytes_accessed=2 * count * aux * window**2,
            transcendentals=0,
        ),
        name="mix",
    )(slots, fitted, received)


def sum_kernel(rows, terms_ref, own_ref, low_ref, high_ref, total):
    peers, listed, ob, lanes = terms_ref.shape
    slab = own_ref.shape[0]
    first = lax.broadcasted_iota(jnp.int32, (ob, lanes), 1) < ob
    total[...] = jnp.zeros_like(total)
    for peer in range(peers):
        for i in range(listed):
            at = peer * 2 * listed + i
            pair = terms_ref[peer, i].astype(F32)
            total[rows[at]] += jnp.where(first, pair, 0.0)
            total[rows[at + listed]] += jnp.where(first, 0.0, pair)

    def folded(rows_of):
        return rows_of[:, :, :ob] + rows_of[:, :, ob:]

    low_ref[...] = folded(total[:HALO])
    high_ref[...] = folded(total[HALO + slab :])
    own_ref[...] = folded(total[HALO : HALO + slab])


def sum_terms(rows, terms, slab):
    ob, lanes = terms.shape[2:]
    shapes = [(slab, ob, ob), (HALO, ob, ob), (HALO, ob, ob)]
    return pl.pallas_call(
        sum_kernel,
        grid_spec=pltpu.PrefetchScalarGridSpec(
            num_scalar_prefetch=1,
            grid=(1,),
            in_specs=[whole(terms.shape)],
            out_specs=[whole(s) for s in shapes],
            scratch_shapes=[pltpu.VMEM((slab + 2 * HALO, ob, lanes), F32)],
        ),
        out_shape=[jax.ShapeDtypeStruct(s, F32) for s in shapes],
        cost_estimate=pl.CostEstimate(flops=0, bytes_accessed=2**21, transcendentals=0),
        name="sum_terms",
    )(rows, terms)


def edge_kernel(own_ref, before_ref, after_ref, out_ref):
    @pl.when(pl.program_id(0) == 0)
    def _():
        out_ref[...] = own_ref[...] + before_ref[...]

    @pl.when(pl.program_id(0) == 1)
    def _():
        out_ref[...] = own_ref[...] + after_ref[...]


def add_edges(own, before, after):
    slab, ob = own.shape[:2]
    last = slab // HALO - 1
    edge = pl.BlockSpec((HALO, ob, ob), lambda e: (e * last, 0, 0))
    return pl.pallas_call(
        edge_kernel,
        grid=(2,),
        in_specs=[edge, whole(before.shape), whole(after.shape)],
        out_specs=edge,
        out_shape=jax.ShapeDtypeStruct(own.shape, F32),
        input_output_aliases={0: 0},
        name="add_edges",
    )(own, before, after)


def ring(value, axis, steps):
    count = lax.axis_size(axis)
    pairs = [(source, (source + steps) % count) for source in range(count)]
    return lax.ppermute(value, axis, pairs)


def per_device(raw_integrals, metric, aux_list, density_list, density_blocks):
    slab, _, ob = density_blocks.shape[:3]
    count, listed = aux_list.shape
    peers = lax.axis_size("dev")
    block_count = slab * lax.axis_size("ta")
    window = listed * ob
    first_block = lax.axis_index("ta") * slab - HALO
    own = density_blocks.reshape(slab, ob, ob)

    names = jnp.broadcast_to(aux_list.reshape(1, -1), (peers, count * listed))
    names = lax.all_to_all(names, "dev", 0, 0, tiled=True)
    rows = ((names - first_block) % block_count).reshape(-1)
    before = ring(own[-HALO:], "ta", 1)
    after = ring(own[:HALO], "ta", -1)

    columns = density_list[aux_list]
    match = columns[:, :, None, :] == aux_list[:, None, :, None]
    places = jnp.arange(1, columns.shape[-1] + 1, dtype=jnp.int32)
    slots = (jnp.sum(jnp.where(match, places, 0), axis=-1) - 1).reshape(-1)

    fitted = fit(raw_integrals, metric, window, 0)
    packed = pack(rows, own, before, after, peers, listed)
    received = lax.all_to_all(packed, "dev", 0, 0, tiled=True)
    fitted = fit(raw_integrals, metric, window, 1, fitted)
    terms = mix(slots, fitted, received)
    terms = lax.all_to_all(terms, "dev", 0, 0, tiled=True)
    totals, low, high = sum_terms(rows, terms, slab)
    from_before = ring(high, "ta", 1)
    from_after = ring(low, "ta", -1)
    return add_edges(totals, from_before, from_after).reshape(density_blocks.shape)


def solution(mesh):
    placed = (
        P(("ta", "dev"), None, None),
        P(("ta", "dev"), None, None),
        P(("ta", "dev"), None),
        P(),
        P("ta", "dev", None, None),
    )
    return jax.shard_map(
        per_device,
        mesh=mesh,
        in_specs=placed,
        out_specs=P("ta", "dev", None, None),
        check_vma=False,
    )
```

time: 924 us -> 90.3 us (0.10)
  the two profiles are of different devices: /device:TPU:8 before, /device:TPU:99 now
where the time goes in v1:
time: 90.3 us; the launch traced here: 89.7 us
  Pallas kernels  36.1 us (40%)
  starting transfers between devices  21 us (23%)
  blocking collectives  15.2 us (17%)
  waiting for transfers between devices  8.76 us (10%)
  local copies, waits for them, and re-layouts  6.92 us (8%)
  other arithmetic  1.58 us (2%)
    pallas_call x2, Pallas kernels, fit(): pl.pallas_call(functools.partial(fit_kernel, rows, stride, window), grid=...  16.8 us
    all_to_all x1, blocking collectives, per_device(): terms = lax.all_to_all(terms, 'dev', 0, 0, tiled=True)  15.2 us
    pallas_call x1, Pallas kernels, mix(): pl.pallas_call(functools.partial(mix_kernel, part, aux // part), grid_spe...  11.4 us
    ppermute x4, starting transfers between devices, ring(): return lax.ppermute(value, axis, pairs)  8.94 us
    ppermute x4, waiting for transfers between devices, ring(): return lax.ppermute(value, axis, pairs)  8.75 us
    all_to_all x1, starting transfers between devices, per_device(): received = lax.all_to_all(packed, 'dev', 0, 0, tiled=True)  6.32 us
    all_to_all x1, starting transfers between devices, per_device(): names = lax.all_to_all(names, 'dev', 0, 0, tiled=True)  5.75 us
    unnamed x12, local copies, waits for them, and re-layouts  3.76 us
  transfers between devices with their start and end apart: 6, of which 3 were waited for; matrix products, arithmetic and copies ran while one was open for 6% of the time, Pallas kernels for 19%

profile of v1, /device:TPU:99, one launch (start us, length us, event | category | flops | bytes accessed | tf_op | source)
XLA Modules:
  0.0 89.7 jit_solution(7667232552246294910)
XLA Ops:
  0.0 0.8 broadcast_in_dim.20
  0.8 0.6 broadcast_in_dim.21
  1.4 5.8 %all-to-all-start = ((s32[8,1,6]{2,1,0:T(1,128)}), s32[8,1,6]{2,1,0:T(1,128)S(1)}, u32[]{:S(2)}, u32[]{:S(2)}) async-start(s32[8,1,6]{2,1,0:T(1,128)} %broadcast_in_dim.21), calls=%async_computation | async-start | bytes 8192 | tf_op jit(solution)/shard_map/all_to_all | solution.py:249
  7.1 0.9 slice_bitcast_fusion
  8.0 4.6 %collective-permute-start = (bf16[4,64,64]{2,1,0:T(8,128)(2,1)S(1)}, bf16[4,64,64]{2,1,0:T(8,128)(2,1)S(1)}, u32[]{:S(2)}, u32[]{:S(2)}) collective-permute-start(bf16[4,64,64]{2,1,0:T(8,128)(2,1)S(1)} %get-tuple-element.12), channel_id=1, source_target_pairs={{0,8},{8,16},{16,24},{24,32},{32,40},{40,48},{48,56},{56,64},{64,7... | collective-permute-start | bytes 98312 | tf_op jit(solution)/shard_map/ppermute | solution.py:236
  12.6 0.0 collective-permute-start.1
  12.6 0.8 copy.22
  13.4 0.7 compare_select_fusion.1
  14.1 0.9 %copy.20 = s32[1024,8]{1,0:T(8,128)S(1)} copy(s32[1024,8]{0,1:T(8,128)} %param.8) | data formatting | bytes 65536 | tf_op args[3]
  15.0 0.1 reshape.31
  15.1 0.6 gather_fusion
  15.8 0.1 sub.21
  15.8 0.5 and_select_fusion.rows
  16.4 0.0 collective-permute-done.before_ref
  16.4 2.0 %collective-permute-done.1.after_ref = bf16[4,64,64]{2,1,0:T(8,128)(2,1)S(1)} collective-permute-done((bf16[4,64,64]{2,1,0:T(8,128)(2,1)S(1)}, bf16[4,64,64]{2,1,0:T(8,128)(2,1)S(1)}, u32[]{:S(2)}, u32[]{:S(2)}) %collective-permute-start.1) | collective-permute-done | bytes 32800 | tf_op jit(solution)/shard_map/ppermute | solution.py:236
  18.4 0.6 copy-done.4
  19.1 2.8 %pack.1 = bf16[8,3,64,128]{3,2,1,0:T(8,128)(2,1)} custom-call(s32[48]{0:T(128)} %and_select_fusion.rows, bf16[32,64,64]{2,1,0:T(8,128)(2,1)} %bitcast.10, bf16[4,64,64]{2,1,0:T(8,128)(2,1)} %copy-done.3, bf16[4,64,64]{2,1,0:T(8,128)(2,1)} %copy-done.4), custom_call_target="tpu_custom_call" | custom-call | bytes 1048576 | tf_op jit(solution)/shard_map/pack/pallas_call | solution.py:81
  21.8 6.3 %all-to-all-start.1 = ((bf16[8,3,64,128]{3,2,1,0:T(8,128)(2,1)}), bf16[8,3,64,128]{3,2,1,0:T(8,128)(2,1)S(1)}, u32[]{:S(2)}, u32[]{:S(2)}) async-start(bf16[8,3,64,128]{3,2,1,0:T(8,128)(2,1)} %pack.1), calls=%async_computation.1 | async-start | bytes 786432 | tf_op jit(solution)/shard_map/all_to_all | solution.py:261
  28.1 0.3 fusion
  28.5 0.1 copy.23
  28.6 0.1 sub.23.slots
  28.7 0.8 copy-done
  29.4 8.4 %fit.2.refs_0_ = bf16[2,64,192,192]{3,2,1,0:T(8,128)(2,1)} custom-call(bf16[2,64,64]{2,1,0:T(8,128)(2,1)S(1)} %copy-done, bf16[2,64,36864]{2,1,0:T(8,128)(2,1)} %raw_ref.3), custom_call_target="tpu_custom_call" | custom-call | flops 301989888 | bytes 11796480 | tf_op jit(solution)/shard_map/fit/pallas_call | solution.py:49
  37.9 8.4 %fit.3.fit_ref = bf16[2,64,192,192]{3,2,1,0:T(8,128)(2,1)} custom-call(bf16[2,64,64]{2,1,0:T(8,128)(2,1)S(1)} %copy-done, bf16[2,64,36864]{2,1,0:T(8,128)(2,1)} %raw_ref.3, bf16[2,64,192,192]{3,2,1,0:T(8,128)(2,1)} %fit.2.refs_0_), custom_call_target="tpu_custom_call", output_to_operand_aliasing={{}: (2, {})} | custom-call | flops 301989888 | bytes 11796480 | tf_op jit(solution)/shard_map/fit/pallas_call | solution.py:49
  46.3 11.4 %mix.1 = bf16[8,3,64,128]{3,2,1,0:T(8,128)(2,1)S(1)} custom-call(s32[18]{0:T(128)S(1)} %sub.23.slots, bf16[2,64,192,192]{3,2,1,0:T(8,128)(2,1)} %fit.3.fit_ref, bf16[8,3,64,128]{3,2,1,0:T(8,128)(2,1)S(1)} %all-to-all-done.1.recv_ref), custom_call_target="tpu_custom_call" | custom-call | flops 3623878656 | bytes 9437184 | tf_op jit(solution)/shard_map/mix/pallas_call | solution.py:147
  57.7 15.2 %all_to_all.16.terms_ref = bf16[8,3,64,128]{3,2,1,0:T(8,128)(2,1)} all-to-all(bf16[8,3,64,128]{3,2,1,0:T(8,128)(2,1)S(1)} %mix.1), channel_id=1, replica_groups=mesh['ta'=32,'dev'=8] {'dev'}, dimensions={0} | all-to-all | bytes 786432 | tf_op jit(solution)/shard_map/all_to_all | solution.py:264
  72.9 3.3 %sum_terms.1 = (f32[32,64,64]{2,1,0:T(8,128)}, f32[4,64,64]{2,1,0:T(8,128)}, f32[4,64,64]{2,1,0:T(8,128)}) custom-call(s32[48]{0:T(128)} %and_select_fusion.rows, bf16[8,3,64,128]{3,2,1,0:T(8,128)(2,1)} %all_to_all.16.terms_ref), custom_call_target="tpu_custom_call" | custom-call | bytes 2097152 | tf_op jit(solution)/shard_map/sum_terms/pallas_call | solution.py:193
  76.2 4.3 %collective-permute-start.2 = (f32[4,64,64]{2,1,0:T(8,128)}, f32[4,64,64]{2,1,0:T(8,128)S(1)}, u32[]{:S(2)}, u32[]{:S(2)}) collective-permute-start(f32[4,64,64]{2,1,0:T(8,128)} %get-tuple-element.9), channel_id=1, source_target_pairs={{0,8},{8,16},{16,24},{24,32},{32,40},{40,48},{48,56},{56,64},{64,7... | collective-permute-start | bytes 196616 | tf_op jit(solution)/shard_map/ppermute | solution.py:236
  80.5 2.3 %collective-permute-done.2.before_ref = f32[4,64,64]{2,1,0:T(8,128)S(1)} collective-permute-done((f32[4,64,64]{2,1,0:T(8,128)}, f32[4,64,64]{2,1,0:T(8,128)S(1)}, u32[]{:S(2)}, u32[]{:S(2)}) %collective-permute-start.2) | collective-permute-done | bytes 65568 | tf_op jit(solution)/shard_map/ppermute | solution.py:236
  82.8 4.4 %collective-permute-done.3.after_ref = f32[4,64,64]{2,1,0:T(8,128)S(1)} collective-permute-done((f32[4,64,64]{2,1,0:T(8,128)}, f32[4,64,64]{2,1,0:T(8,128)S(1)}, u32[]{:S(2)}, u32[]{:S(2)}) %collective-permute-start.3) | collective-permute-done | bytes 65568 | tf_op jit(solution)/shard_map/ppermute | solution.py:236
  87.3 0.6 copy-done.2
  87.9 1.8 %add_edges.1 = f32[32,64,64]{2,1,0:T(8,128)} custom-call(f32[32,64,64]{2,1,0:T(8,128)} %get-tuple-element.8.own_ref, f32[4,64,64]{2,1,0:T(8,128)} %copy-done.1, f32[4,64,64]{2,1,0:T(8,128)} %copy-done.2), custom_call_target="tpu_custom_call", output_to_operand_aliasing={{}: (0, {})} | custom-call | tf_op jit(solution)/shard_map/add_edges/pallas_call | solution.py:222
  (16 shorter events, 0.1 us)
Async XLA Ops:
  1.4 14.4 %all-to-all-start = ((s32[8,1,6]{2,1,0:T(1,128)}), s32[8,1,6]{2,1,0:T(1,128)S(1)}, u32[]{:S(2)}, u32[]{:S(2)}) async-start(s32[8,1,6]{2,1,0:T(1,128)} %broadcast_in_dim.21), calls=%async_computation | async-start | bytes 8192 | tf_op jit(solution)/shard_map/all_to_all | solution.py:249
  8.0 8.4 %collective-permute-start = (bf16[4,64,64]{2,1,0:T(8,128)(2,1)S(1)}, bf16[4,64,64]{2,1,0:T(8,128)(2,1)S(1)}, u32[]{:S(2)}, u32[]{:S(2)}) collective-permute-start(bf16[4,64,64]{2,1,0:T(8,128)(2,1)S(1)} %get-tuple-element.12), channel_id=1, source_target_pairs={{0,8},{8,16},{16,24},{24,32},{32,40},{40,48},{48,56},{56,64},{64,7... | collective-permute-start | bytes 98312 | tf_op jit(solution)/shard_map/ppermute | solution.py:236
  12.6 5.8 %collective-permute-start.1 = (bf16[4,64,64]{2,1,0:T(8,128)(2,1)S(1)}, bf16[4,64,64]{2,1,0:T(8,128)(2,1)S(1)}, u32[]{:S(2)}, u32[]{:S(2)}) collective-permute-start(bf16[4,64,64]{2,1,0:T(8,128)(2,1)S(1)} %get-tuple-element.11), channel_id=1, source_target_pairs={{0,248},{8,0},{16,8},{24,16},{32,24},{40,32},{48,40},{56,48},{64,5... | collective-permute-start | bytes 98312 | tf_op jit(solution)/shard_map/ppermute | solution.py:236
  16.4 2.1 %copy-start.3 = (bf16[4,64,64]{2,1,0:T(8,128)(2,1)}, bf16[4,64,64]{2,1,0:T(8,128)(2,1)S(1)}, u32[]{:S(2)}) copy-start(bf16[4,64,64]{2,1,0:T(8,128)(2,1)S(1)} %collective-permute-done.before_ref) | copy-start | bytes 98308
  18.4 0.6 copy-start.4
  21.8 24.4 %all-to-all-start.1 = ((bf16[8,3,64,128]{3,2,1,0:T(8,128)(2,1)}), bf16[8,3,64,128]{3,2,1,0:T(8,128)(2,1)S(1)}, u32[]{:S(2)}, u32[]{:S(2)}) async-start(bf16[8,3,64,128]{3,2,1,0:T(8,128)(2,1)} %pack.1), calls=%async_computation.1 | async-start | bytes 786432 | tf_op jit(solution)/shard_map/all_to_all | solution.py:261
  28.7 0.8 copy-start
  76.2 6.6 %collective-permute-start.2 = (f32[4,64,64]{2,1,0:T(8,128)}, f32[4,64,64]{2,1,0:T(8,128)S(1)}, u32[]{:S(2)}, u32[]{:S(2)}) collective-permute-start(f32[4,64,64]{2,1,0:T(8,128)} %get-tuple-element.9), channel_id=1, source_target_pairs={{0,8},{8,16},{16,24},{24,32},{32,40},{40,48},{48,56},{56,64},{64,7... | collective-permute-start | bytes 196616 | tf_op jit(solution)/shard_map/ppermute | solution.py:236
  80.5 6.7 %collective-permute-start.3 = (f32[4,64,64]{2,1,0:T(8,128)}, f32[4,64,64]{2,1,0:T(8,128)S(1)}, u32[]{:S(2)}, u32[]{:S(2)}) collective-permute-start(f32[4,64,64]{2,1,0:T(8,128)} %get-tuple-element.10), channel_id=1, source_target_pairs={{0,248},{8,0},{16,8},{24,16},{32,24},{40,32},{48,40},{56,48},{64,5... | collective-permute-start | bytes 196616 | tf_op jit(solution)/shard_map/ppermute | solution.py:236
  82.8 4.5 %copy-start.1 = (f32[4,64,64]{2,1,0:T(8,128)}, f32[4,64,64]{2,1,0:T(8,128)S(1)}, u32[]{:S(2)}) copy-start(f32[4,64,64]{2,1,0:T(8,128)S(1)} %collective-permute-done.2.before_ref) | copy-start | bytes 196612
  87.2 0.7 copy-start.2

commit v2 on v0

v2 whole, which is shorter than its diff:
```python
import functools

import jax
import jax.numpy as jnp
from jax import lax
from jax.experimental import pallas as pl
from jax.experimental.pallas import tpu as pltpu
from jax.sharding import PartitionSpec as P

BF16 = jnp.bfloat16
F32 = jnp.float32
HALO = 4
PAIRS = 32
STEP = 32
DEPTH = 3
PIECE = 16
PARTS = ((16, 16, 32), (32, 32))
VMEM_LIMIT = 56 * 2**20


def in_vmem():
    return pl.BlockSpec(memory_space=pltpu.VMEM)


def in_smem():
    return pl.BlockSpec(memory_space=pltpu.SMEM)


def anywhere():
    return pl.BlockSpec(memory_space=pl.ANY)


def fit_kernel(pairs, stride, names, columns, metric_ref, raw_ref, out_ref, slots, *refs):
    held, made, in_sems, out_sems, *parts = refs
    count, aux = metric_ref.shape[:2]
    rows, width = out_ref.shape[2:]
    pieces = rows // STEP
    total = count * pieces
    chunks = count * rows // pairs

    def arriving(k):
        slot = k % DEPTH
        lanes = pl.ds(k % pieces * STEP * width, STEP * width)
        there = raw_ref.at[k // pieces, :, lanes]
        return pltpu.make_async_copy(there, held.at[slot], in_sems.at[slot])

    def leaving(n):
        a, start = divmod(n * pairs, rows)
        there = out_ref.at[a, :, pl.ds(start, pairs), :]
        return pltpu.make_async_copy(made.at[n % 2], there, out_sems.at[n % 2])

    for k in range(DEPTH):
        arriving(k).start()
    stored, listed = columns.shape[0], names.shape[1]
    for a in range(count):
        for i in range(listed):
            row = names[a, i]
            for j in range(listed):
                column = names[a, j]
                slot = jnp.int32(-1)
                for k in range(stored):
                    slot = jnp.where(columns[k, row] == column, k, slot)
                slots[(a * listed + i) * listed + j] = slot
    for n in range(chunks):
        metric = metric_ref[n * pairs // rows]
        for r in range(pairs):
            k, at = divmod(n * pairs + r, STEP)
            if at == 0:
                arriving(k).wait()
            lanes = pl.ds(at * width, width)
            both = jnp.dot(metric, held[k % DEPTH, :, lanes], preferred_element_type=F32)
            for v, part in enumerate(parts):
                part[pl.ds(r, aux, stride=stride), :] = both[:, v * 128 : (v + 1) * 128]
            if at == STEP - 1 and k + DEPTH < total:
                arriving(k + DEPTH).start()
        if n >= 2:
            leaving(n - 2).wait()
        for v, part in enumerate(parts):
            values = part[...].reshape(aux, stride, 128)[:, :pairs]
            made[n % 2, :, :, v * 128 : (v + 1) * 128] = values.astype(BF16)
        leaving(n).start()
    for n in range(chunks - 2, chunks):
        leaving(n).wait()


def fit(names, columns, metric, raw, window):
    count, aux, merged = raw.shape
    listed = names.shape[1]
    stride = PAIRS + 8
    width = 2 * window
    return pl.pallas_call(
        functools.partial(fit_kernel, PAIRS, stride),
        in_specs=[in_smem(), in_smem(), in_vmem(), anywhere()],
        out_specs=[anywhere(), in_smem()],
        out_shape=[
            jax.ShapeDtypeStruct((count, aux, window // 2, width), BF16),
            jax.ShapeDtypeStruct((count * listed * listed,), jnp.int32),
        ],
        scratch_shapes=[
            pltpu.VMEM((DEPTH, aux, STEP * width), BF16),
            pltpu.VMEM((2, aux, PAIRS, width), BF16),
            pltpu.SemaphoreType.DMA((DEPTH,)),
            pltpu.SemaphoreType.DMA((2,)),
        ]
        + [pltpu.VMEM((aux * stride, 128), F32)] * (width // 128),
        compiler_params=pltpu.CompilerParams(vmem_limit_bytes=VMEM_LIMIT),
        cost_estimate=pl.CostEstimate(
            flops=2 * count * aux * aux * merged,
            bytes_accessed=4 * count * aux * merged,
            transcendentals=0,
        ),
        name="fit",
    )(names, columns, metric, raw)


def pack_kernel(rows, own_ref, before_ref, after_ref, out_ref, near):
    slab = own_ref.shape[0]
    near[:HALO] = before_ref[...]
    near[HALO : HALO + slab] = own_ref[...]
    near[HALO + slab :] = after_ref[...]
    peers, listed = out_ref.shape[:2]
    for peer in range(peers):
        for i in range(listed):
            pair = [near[rows[peer, a, i]] for a in range(2)]
            out_ref[peer, i] = jnp.concatenate(pair, axis=1)


def pack(rows, own, before, after):
    slab, ob = own.shape[:2]
    peers, _, listed = rows.shape
    return pl.pallas_call(
        pack_kernel,
        in_specs=[in_smem(), in_vmem(), in_vmem(), in_vmem()],
        out_specs=in_vmem(),
        scratch_shapes=[pltpu.VMEM((slab + 2 * HALO, ob, ob), BF16)],
        out_shape=jax.ShapeDtypeStruct((peers, listed, ob, 2 * ob), BF16),
        cost_estimate=pl.CostEstimate(flops=0, bytes_accessed=2**20, transcendentals=0),
        name="pack",
    )(rows, own, before, after)


def mix_kernel(slots, fit_ref, recv_ref, out_ref, dens, held, sems):
    count, aux, pairs, width = fit_ref.shape
    listed, ob = recv_ref.shape[1:3]
    window = width // 2
    total = count * aux // PIECE

    def arriving(n):
        at = (n * PIECE // aux, pl.ds(n * PIECE % aux, PIECE))
        return pltpu.make_async_copy(fit_ref.at[at], held.at[at], sems.at[n])

    for n in range(DEPTH):
        arriving(n).start()
    out_ref[...] = jnp.zeros_like(out_ref)
    row = lax.broadcasted_iota(jnp.int32, (window, window), 0)
    column = lax.broadcasted_iota(jnp.int32, (window, window), 1)
    turn = (lax.rem(row, 2) * pairs + lax.div(row, 2) == column).astype(BF16)
    across = (((1,), (1,)), ((), ()))
    for a in range(count):
        for i in range(listed):
            blocks = []
            for j in range(listed):
                slot = slots[(a * listed + i) * listed + j]
                block = recv_ref[jnp.maximum(slot, 0), i, :, a * ob : (a + 1) * ob]
                blocks.append(jnp.where(slot >= 0, block, jnp.zeros_like(block)))
            dens[a, i * ob : (i + 1) * ob, :] = jnp.concatenate(blocks, axis=1)
    for a in range(count):
        density = dens[a]
        summed = None
        done = 0
        for part in PARTS[a]:
            for n in range((a * aux + done) // PIECE, (a * aux + done + part) // PIECE):
                arriving(n).wait()
                if n + DEPTH < total:
                    arriving(n + DEPTH).start()
            rows = held[a, pl.ds(done, part)]
            fitted = jnp.concatenate([rows[..., :window], rows[..., window:]], axis=1)
            fitted = fitted.reshape(part * window, window)
            mixed = jnp.dot(fitted, density, preferred_element_type=F32).astype(BF16)
            for q in range(part):
                at = slice(q * window, (q + 1) * window)
                term = lax.dot_general(
                    mixed[at], fitted[at], across, preferred_element_type=F32
                )
                summed = term if summed is None else summed + term
            done += part

        half = lax.dot_general(
            summed.astype(BF16), turn, across, preferred_element_type=F32
        ).astype(BF16)
        terms = jnp.dot(turn, half, preferred_element_type=F32).astype(BF16)
        for i in range(listed):
            for j in range(listed):
                slot = slots[(a * listed + i) * listed + j]
                block = terms[i * ob : (i + 1) * ob, j * ob : (j + 1) * ob]

                @pl.when(slot >= 0)
                def _():
                    out_ref[slot, i, :, a * ob : (a + 1) * ob] = block


def mix(slots, fitted, received):
    count, aux, pairs, width = fitted.shape
    window = width // 2
    return pl.pallas_call(
        mix_kernel,
        in_specs=[in_smem(), anywhere(), in_vmem()],
        out_specs=in_vmem(),
        scratch_shapes=[
            pltpu.VMEM((count, window, window), BF16),
            pltpu.VMEM(fitted.shape, BF16),
            pltpu.SemaphoreType.DMA((count * aux // PIECE,)),
        ],
        out_shape=jax.ShapeDtypeStruct(received.shape, BF16),
        compiler_params=pltpu.CompilerParams(vmem_limit_bytes=VMEM_LIMIT),
        cost_estimate=pl.CostEstimate(
            flops=4 * count * aux * window**3,
            bytes_accessed=2 * count * aux * window**2,
            transcendentals=0,
        ),
        name="mix",
    )(slots, fitted, received)


def halves(pair):
    first = lax.broadcasted_iota(jnp.int32, pair.shape, 1) < pair.shape[1] // 2
    return jnp.where(first, pair, 0.0), jnp.where(first, 0.0, pair)


def folded(pair):
    ob = pair.shape[-1] // 2
    return pair[..., :ob] + pair[..., ob:]


def halo_kernel(slab, rows, terms_ref, low_ref, high_ref, total):
    peers, listed, ob, _ = terms_ref.shape
    total[...] = jnp.zeros_like(total)
    for peer in range(peers):
        for i in range(listed):
            for a in range(2):
                row = rows[peer, a, i]

                @pl.when((row < HALO) | (row >= HALO + slab))
                def _():
                    at = jnp.where(row < HALO, row, row - slab)
                    total[at] += halves(terms_ref[peer, i].astype(F32))[a]

    for ref, start in ((low_ref, 0), (high_ref, HALO)):
        sums = folded(total[start : start + HALO])
        for h in range(HALO // 2):
            ref[h] = jnp.concatenate([sums[h], sums[h + HALO // 2]], axis=1)


def halo_sums(slab, rows, terms):
    ob, lanes = terms.shape[2:]
    shape = jax.ShapeDtypeStruct((HALO // 2, ob, lanes), F32)
    return pl.pallas_call(
        functools.partial(halo_kernel, slab),
        in_specs=[in_smem(), in_vmem()],
        out_specs=[in_vmem(), in_vmem()],
        scratch_shapes=[pltpu.VMEM((2 * HALO, ob, lanes), F32)],
        out_shape=[shape, shape],
        cost_estimate=pl.CostEstimate(flops=0, bytes_accessed=2**19, transcendentals=0),
        name="halo_sums",
    )(rows, terms)


def own_kernel(rows, terms_ref, own_ref, edge_ref, total):
    peers, listed, ob, _ = terms_ref.shape
    slab = own_ref.shape[0]
    total[...] = jnp.zeros_like(total)
    for peer in range(peers):
        for i in range(listed):
            pair = halves(terms_ref[peer, i].astype(F32))
            for a in range(2):
                total[rows[peer, a, i]] += pair[a]
    sums = folded(total[HALO : HALO + slab])
    own_ref[...] = sums
    edge_ref[:HALO] = sums[:HALO]
    edge_ref[HALO:] = sums[slab - HALO :]


def own_sums(slab, rows, terms):
    ob, lanes = terms.shape[2:]
    return pl.pallas_call(
        own_kernel,
        in_specs=[in_smem(), in_vmem()],
        out_specs=[in_vmem(), in_vmem()],
        scratch_shapes=[pltpu.VMEM((slab + 2 * HALO, ob, lanes), F32)],
        out_shape=[
            jax.ShapeDtypeStruct((slab, ob, ob), F32),
            jax.ShapeDtypeStruct((2 * HALO, ob, ob), F32),
        ],
        cost_estimate=pl.CostEstimate(flops=0, bytes_accessed=2**21, transcendentals=0),
        name="own_sums",
    )(rows, terms)


def edge_kernel(own_ref, edge_ref, before_ref, after_ref, out_ref, rows, sems):
    del own_ref
    slab, ob = out_ref.shape[:2]
    copies = []
    for side, (ref, start) in enumerate(((before_ref, 0), (after_ref, slab - HALO))):
        at = pl.ds(side * HALO, HALO)
        for h in range(HALO):
            lanes = slice(h // 2 * ob, (h // 2 + 1) * ob)
            rows[side * HALO + h] = edge_ref[side * HALO + h] + ref[h % 2, :, lanes]
        copies.append(
            pltpu.make_async_copy(rows.at[at], out_ref.at[pl.ds(start, HALO)], sems.at[side])
        )
        copies[-1].start()
    for copy in copies:
        copy.wait()


def add_edges(own, edges, before, after):
    return pl.pallas_call(
        edge_kernel,
        in_specs=[pl.BlockSpec(memory_space=pl.ANY), in_vmem(), in_vmem(), in_vmem()],
        out_specs=pl.BlockSpec(memory_space=pl.ANY),
        out_shape=jax.ShapeDtypeStruct(own.shape, F32),
        scratch_shapes=[pltpu.VMEM(edges.shape, F32), pltpu.SemaphoreType.DMA((2,))],
        input_output_aliases={0: 0},
        name="add_edges",
    )(own, edges, before, after)


def ring(value, axis, steps):
    count = lax.axis_size(axis)
    pairs = [(source, (source + steps) % count) for source in range(count)]
    return lax.ppermute(value, axis, pairs)


def per_device(raw_integrals, metric, aux_list, density_list, density_blocks):
    slab, _, ob = density_blocks.shape[:3]
    count, listed = aux_list.shape
    peers = lax.axis_size("dev")
    block_count = slab * lax.axis_size("ta")
    first = lax.axis_index("ta") * slab - HALO
    own = density_blocks.reshape(slab, ob, ob)

    names = jnp.broadcast_to(aux_list[None], (peers, count, listed))
    names = lax.all_to_all(names, "dev", 0, 0, tiled=True)

    rows = (names - first) % block_count
    before = ring(own[-HALO:], "ta", 1)
    after = ring(own[:HALO], "ta", -1)

    packed = pack(rows, own, before, after)
    received = lax.all_to_all(packed, "dev", 0, 0, tiled=True)
    fitted, slots = fit(aux_list, density_list.T, metric, raw_integrals, listed * ob)
    terms = mix(slots, fitted, received)
    terms = lax.all_to_all(terms, "dev", 0, 0, tiled=True)
    low, high = halo_sums(slab, rows, terms)
    from_before = ring(high, "ta", 1)
    from_after = ring(low, "ta", -1)
    totals, edges = own_sums(slab, rows, terms)
    return add_edges(totals, edges, from_before, from_after).reshape(density_blocks.shape)


def solution(mesh):
    placed = (
        P(("ta", "dev"), None, None),
        P(("ta", "dev"), None, None),
        P(("ta", "dev"), None),
        P(),
        P("ta", "dev", None, None),
    )
    return jax.shard_map(
        per_device,
        mesh=mesh,
        in_specs=placed,
        out_specs=P("ta", "dev", None, None),
        check_vma=False,
    )
```

time: 924 us -> 82.4 us (0.09)
  waiting for transfers between devices: 653 us -> 5.19 us
  local copies, waits for them, and re-layouts: 126 us -> 4.16 us
  matrix products: 53.7 us -> 0 us
  Pallas kernels: 0 us -> 32.3 us
  other arithmetic: 27.4 us -> 0.61 us
  starting transfers between devices: 47.2 us -> 23.9 us
  blocking collectives: 0 us -> 15.5 us
  between operations: 13.4 us -> 0.22 us
    unnamed x3 -> x0, waiting for transfers between devices: 433 us -> none
    ppermute x4, waiting for transfers between devices: 140 us -> 4.68 us  [ring(): return lax.ppermute(value, axis, pairs)]
    reshape x10 -> x0, local copies, waits for them, and re-layouts: 88.2 us -> none  [the longest x4 44.9 us: block_terms(): mixed = mixed.astype(jnp.bfloat16).reshape(functions, window, window)]
    all_gather x1 -> x0, waiting for transfers between devices: 80.8 us -> none  [per_device(): panel_rows = lax.all_gather(density_blocks, 'dev', axis=1, tiled=True)]
    dot_general x10 -> x0, matrix products: 53.7 us -> none  [the longest x2 26.1 us: block_terms(): lax.dot_general(mixed, fitted, (((0, 2), (0, 2)), ((), ())), preferred_el...]
    ppermute x4, starting transfers between devices: 47.2 us -> 8.7 us  [ring(): return lax.ppermute(value, axis, pairs)]
    pallas_call x0 -> x6, Pallas kernels: none -> 32.3 us  [the longest x1 12.3 us: mix(): pl.pallas_call(mix_kernel, in_specs=[in_smem(), anywhere(), in_vmem()], o...]
    all_to_all x0 -> x1, blocking collectives: none -> 15.5 us  [per_device(): terms = lax.all_to_all(terms, 'dev', 0, 0, tiled=True)]
  transfers between devices with their start and end apart: 6 -> 6, of which waited for: 5 -> 3; matrix products, arithmetic and copies ran while one was open for 0% -> 2% of each run, Pallas kernels for 0% -> 17%
where the time goes in v2:
time: 82.4 us; the launch traced here: 81.8 us
  Pallas kernels  32.3 us (39%)
  starting transfers between devices  23.9 us (29%)
  blocking collectives  15.5 us (19%)
  waiting for transfers between devices  5.19 us (6%)
  local copies, waits for them, and re-layouts  4.16 us (5%)
    all_to_all x1, blocking collectives, per_device(): terms = lax.all_to_all(terms, 'dev', 0, 0, tiled=True)  15.5 us
    pallas_call x1, Pallas kernels, mix(): pl.pallas_call(mix_kernel, in_specs=[in_smem(), anywhere(), in_vmem()], o...  12.3 us
    pallas_call x1, Pallas kernels, fit(): pl.pallas_call(functools.partial(fit_kernel, PAIRS, stride), in_specs=[in...  11.1 us
    ppermute x4, starting transfers between devices, ring(): return lax.ppermute(value, axis, pairs)  8.7 us
    all_to_all x1, starting transfers between devices, per_device(): received = lax.all_to_all(packed, 'dev', 0, 0, tiled=True)  7.81 us
    all_to_all x1, starting transfers between devices, per_device(): names = lax.all_to_all(names, 'dev', 0, 0, tiled=True)  7.38 us
    ppermute x4, waiting for transfers between devices, ring(): return lax.ppermute(value, axis, pairs)  4.68 us
    pallas_call x1, Pallas kernels, own_sums(): pl.pallas_call(own_kernel, in_specs=[in_smem(), in_vmem()], out_specs=[in...  2.7 us
  transfers between devices with their start and end apart: 6, of which 3 were waited for; matrix products, arithmetic and copies ran while one was open for 2% of the time, Pallas kernels for 17%

profile of v2, /device:TPU:8, one launch (start us, length us, event | category | flops | bytes accessed | tf_op | source)
XLA Modules:
  0.0 81.8 jit_solution(6959406417232598627)
XLA Ops:
  0.0 1.3 %broadcast_in_dim.2 = s32[8,2,3]{2,1,0:T(2,128)} broadcast(s32[2,3]{1,0:T(2,128)} %names.1), dimensions={1,2} | broadcast | bytes 216 | tf_op jit(solution)/shard_map/broadcast_in_dim | solution.py:342
  1.3 7.4 %all-to-all-start = ((s32[8,2,3]{2,1,0:T(2,128)}), s32[8,2,3]{2,1,0:T(2,128)S(1)}, u32[]{:S(2)}, u32[]{:S(2)}) async-start(s32[8,2,3]{2,1,0:T(2,128)} %broadcast_in_dim.2), calls=%async_computation | async-start | bytes 16384 | tf_op jit(solution)/shard_map/all_to_all | solution.py:343
  8.7 0.9 %slice_bitcast_fusion = (bf16[4,64,64]{2,1,0:T(8,128)(2,1)S(1)}, bf16[4,64,64]{2,1,0:T(8,128)(2,1)S(1)}) fusion(bf16[32,1,64,64]{3,2,0,1:T(8,128)(2,1)} %bitcast.10), kind=kLoop, calls=%fused_computation | loop fusion | bytes 131072 | tf_op jit(solution)/shard_map/slice | solution.py:347
  9.5 4.8 %collective-permute-start.1 = (bf16[4,64,64]{2,1,0:T(8,128)(2,1)S(1)}, bf16[4,64,64]{2,1,0:T(8,128)(2,1)S(1)}, u32[]{:S(2)}, u32[]{:S(2)}) collective-permute-start(bf16[4,64,64]{2,1,0:T(8,128)(2,1)S(1)} %get-tuple-element.17), channel_id=1, source_target_pairs={{0,248},{8,0},{16,8},{24,16},{32,24},{40,32},{48,40},{56,48},{64,5... | collective-permute-start | bytes 98312 | tf_op jit(solution)/shard_map/ppermute | solution.py:331
  14.4 0.0 collective-permute-start
  14.4 0.5 all-to-all-done
  14.9 0.6 and_select_fusion.rows
  15.5 0.8 collective-permute-done.1.after_ref
  16.3 0.0 copy-start.1
  16.3 3.9 %collective-permute-done.before_ref = bf16[4,64,64]{2,1,0:T(8,128)(2,1)S(1)} collective-permute-done((bf16[4,64,64]{2,1,0:T(8,128)(2,1)S(1)}, bf16[4,64,64]{2,1,0:T(8,128)(2,1)S(1)}, u32[]{:S(2)}, u32[]{:S(2)}) %collective-permute-start) | collective-permute-done | bytes 32800 | tf_op jit(solution)/shard_map/ppermute | solution.py:331
  20.2 0.0 copy-start.2
  20.2 0.0 copy-done.1
  20.2 0.6 copy-done.2
  20.8 2.1 %pack.1 = bf16[8,3,64,128]{3,2,1,0:T(8,128)(2,1)} custom-call(s32[8,2,3]{2,1,0:T(2,128)} %and_select_fusion.rows, bf16[32,64,64]{2,1,0:T(8,128)(2,1)} %bitcast.11, bf16[4,64,64]{2,1,0:T(8,128)(2,1)} %copy-done.2, bf16[4,64,64]{2,1,0:T(8,128)(2,1)} %copy-done.1), custom_call_target="tpu_custom_call" | custom-call | bytes 1048576 | tf_op jit(solution)/shard_map/pack/pallas_call | solution.py:131
  22.9 7.8 %all-to-all-start.1 = ((bf16[8,3,64,128]{3,2,1,0:T(8,128)(2,1)}), bf16[8,3,64,128]{3,2,1,0:T(8,128)(2,1)S(1)}, u32[]{:S(2)}, u32[]{:S(2)}) async-start(bf16[8,3,64,128]{3,2,1,0:T(8,128)(2,1)} %pack.1), calls=%async_computation.1 | async-start | bytes 786432 | tf_op jit(solution)/shard_map/all_to_all | solution.py:350
  30.7 11.1 %fit.1 = (bf16[2,64,96,384]{3,2,1,0:T(8,128)(2,1)}, s32[18]{0:T(128)}) custom-call(s32[2,3]{1,0:T(2,128)} %names.1, s32[8,1024]{1,0:T(8,128)} %bitcast.12, bf16[2,64,64]{2,1,0:T(8,128)(2,1)} %metric_ref.1, bf16[2,64,36864]{2,1,0:T(8,128)(2,1)} %raw_ref.1), custom_call_target="tpu_custom_call" | custom-call | flops 603979776 | bytes 18874368 | tf_op jit(solution)/shard_map/fit/pallas_call | solution.py:91
  41.8 0.0 all-to-all-done.1.recv_ref
  41.8 0.0 copy-start
  41.9 0.7 copy-done
  42.6 12.3 %mix.1 = bf16[8,3,64,128]{3,2,1,0:T(8,128)(2,1)} custom-call(s32[18]{0:T(128)} %get-tuple-element.11.slots, bf16[2,64,96,384]{3,2,1,0:T(8,128)(2,1)} %get-tuple-element.12.fit_ref, bf16[8,3,64,128]{3,2,1,0:T(8,128)(2,1)} %copy-done), custom_call_target="tpu_custom_call" | custom-call | flops 3623878656 | bytes 9437184 | tf_op jit(solution)/shard_map/mix/pallas_call | solution.py:205
  54.9 15.5 %all_to_all.15.terms_ref = bf16[8,3,64,128]{3,2,1,0:T(8,128)(2,1)} all-to-all(bf16[8,3,64,128]{3,2,1,0:T(8,128)(2,1)} %mix.1), channel_id=1, replica_groups=mesh['ta'=32,'dev'=8] {'dev'}, dimensions={0} | all-to-all | bytes 786432 | tf_op jit(solution)/shard_map/all_to_all | solution.py:353
  70.4 2.3 %halo_sums.1 = (f32[2,64,128]{2,1,0:T(8,128)}, f32[2,64,128]{2,1,0:T(8,128)}) custom-call(s32[8,2,3]{2,1,0:T(2,128)} %and_select_fusion.rows, bf16[8,3,64,128]{3,2,1,0:T(8,128)(2,1)} %all_to_all.15.terms_ref), custom_call_target="tpu_custom_call" | custom-call | bytes 524288 | tf_op jit(solution)/shard_map/halo_sums/pallas_call | solution.py:257
  72.7 0.0 collective-permute-start.2
  72.7 3.9 %collective-permute-start.3 = (f32[2,64,128]{2,1,0:T(8,128)}, f32[2,64,128]{2,1,0:T(8,128)S(1)}, u32[]{:S(2)}, u32[]{:S(2)}) collective-permute-start(f32[2,64,128]{2,1,0:T(8,128)} %get-tuple-element.16), channel_id=1, source_target_pairs={{0,248},{8,0},{16,8},{24,16},{32,24},{40,32},{48,40},{56,48},{64,5... | collective-permute-start | bytes 196616 | tf_op jit(solution)/shard_map/ppermute | solution.py:331
  76.5 2.7 %own_sums.1 = (f32[32,64,64]{2,1,0:T(8,128)}, f32[8,64,64]{2,1,0:T(8,128)}) custom-call(s32[8,2,3]{2,1,0:T(2,128)} %and_select_fusion.rows, bf16[8,3,64,128]{3,2,1,0:T(8,128)(2,1)} %all_to_all.15.terms_ref), custom_call_target="tpu_custom_call" | custom-call | bytes 2097152 | tf_op jit(solution)/shard_map/own_sums/pallas_call | solution.py:285
  79.2 0.0 collective-permute-done.2.before_ref
  79.2 0.0 copy-start.3
  79.2 0.0 collective-permute-done.3.after_ref
  79.2 0.0 copy-start.4
  79.2 0.6 copy-done.3
  79.8 0.0 copy-done.4
  79.9 1.8 %add_edges.1 = f32[32,64,64]{2,1,0:T(8,128)} custom-call(f32[32,64,64]{2,1,0:T(8,128)} %get-tuple-element.13.own_ref, f32[8,64,64]{2,1,0:T(8,128)} %get-tuple-element.14.edge_ref, f32[2,64,128]{2,1,0:T(8,128)} %copy-done.3, f32[2,64,128]{2,1,0:T(8,128)} %copy-done.4), custom_call_target="tpu_custom_call", output_to_operand_aliasing={{}: (0, {})} | custom-call | tf_op jit(solution)/shard_map/add_edges/pallas_call | solution.py:317
Async XLA Ops:
  1.3 13.6 %all-to-all-start = ((s32[8,2,3]{2,1,0:T(2,128)}), s32[8,2,3]{2,1,0:T(2,128)S(1)}, u32[]{:S(2)}, u32[]{:S(2)}) async-start(s32[8,2,3]{2,1,0:T(2,128)} %broadcast_in_dim.2), calls=%async_computation | async-start | bytes 16384 | tf_op jit(solution)/shard_map/all_to_all | solution.py:343
  9.5 6.7 %collective-permute-start.1 = (bf16[4,64,64]{2,1,0:T(8,128)(2,1)S(1)}, bf16[4,64,64]{2,1,0:T(8,128)(2,1)S(1)}, u32[]{:S(2)}, u32[]{:S(2)}) collective-permute-start(bf16[4,64,64]{2,1,0:T(8,128)(2,1)S(1)} %get-tuple-element.17), channel_id=1, source_target_pairs={{0,248},{8,0},{16,8},{24,16},{32,24},{40,32},{48,40},{56,48},{64,5... | collective-permute-start | bytes 98312 | tf_op jit(solution)/shard_map/ppermute | solution.py:331
  14.4 5.8 %collective-permute-start = (bf16[4,64,64]{2,1,0:T(8,128)(2,1)S(1)}, bf16[4,64,64]{2,1,0:T(8,128)(2,1)S(1)}, u32[]{:S(2)}, u32[]{:S(2)}) collective-permute-start(bf16[4,64,64]{2,1,0:T(8,128)(2,1)S(1)} %get-tuple-element.18), channel_id=1, source_target_pairs={{0,8},{8,16},{16,24},{24,32},{32,40},{40,48},{48,56},{56,64},{64,7... | collective-permute-start | bytes 98312 | tf_op jit(solution)/shard_map/ppermute | solution.py:331
  16.3 3.9 %copy-start.1 = (bf16[4,64,64]{2,1,0:T(8,128)(2,1)}, bf16[4,64,64]{2,1,0:T(8,128)(2,1)S(1)}, u32[]{:S(2)}) copy-start(bf16[4,64,64]{2,1,0:T(8,128)(2,1)S(1)} %collective-permute-done.1.after_ref) | copy-start | bytes 98308
  20.2 0.6 copy-start.2
  22.9 18.9 %all-to-all-start.1 = ((bf16[8,3,64,128]{3,2,1,0:T(8,128)(2,1)}), bf16[8,3,64,128]{3,2,1,0:T(8,128)(2,1)S(1)}, u32[]{:S(2)}, u32[]{:S(2)}) async-start(bf16[8,3,64,128]{3,2,1,0:T(8,128)(2,1)} %pack.1), calls=%async_computation.1 | async-start | bytes 786432 | tf_op jit(solution)/shard_map/all_to_all | solution.py:350
  41.8 0.7 copy-start
  72.7 6.6 %collective-permute-start.2 = (f32[2,64,128]{2,1,0:T(8,128)}, f32[2,64,128]{2,1,0:T(8,128)S(1)}, u32[]{:S(2)}, u32[]{:S(2)}) collective-permute-start(f32[2,64,128]{2,1,0:T(8,128)} %get-tuple-element.15), channel_id=1, source_target_pairs={{0,8},{8,16},{16,24},{24,32},{32,40},{40,48},{48,56},{56,64},{64,7... | collective-permute-start | bytes 196616 | tf_op jit(solution)/shard_map/ppermute | solution.py:331
  72.7 6.6 %collective-permute-start.3 = (f32[2,64,128]{2,1,0:T(8,128)}, f32[2,64,128]{2,1,0:T(8,128)S(1)}, u32[]{:S(2)}, u32[]{:S(2)}) collective-permute-start(f32[2,64,128]{2,1,0:T(8,128)} %get-tuple-element.16), channel_id=1, source_target_pairs={{0,248},{8,0},{16,8},{24,16},{32,24},{40,32},{48,40},{56,48},{64,5... | collective-permute-start | bytes 196616 | tf_op jit(solution)/shard_map/ppermute | solution.py:331
  79.2 0.6 copy-start.3
  79.2 0.6 copy-start.4

commit v3 on v2

--- a/solution.py
+++ b/solution.py
@@ -26,12 +26,16 @@
     return pl.BlockSpec(memory_space=pltpu.SMEM)
 
 
+def held_in_vmem(value):
+    return pltpu.with_memory_space_constraint(value, pltpu.VMEM)
+
+
 def anywhere():
     return pl.BlockSpec(memory_space=pl.ANY)
 
 
-def fit_kernel(pairs, stride, names, columns, metric_ref, raw_ref, out_ref, slots, *refs):
-    held, made, in_sems, out_sems, *parts = refs
+def fit_kernel(pairs, stride, names, columns_ref, metric_ref, raw_ref, out_ref, slots, *refs):
+    held, made, in_sems, out_sems, columns, listing, *parts = refs
     count, aux = metric_ref.shape[:2]
     rows, width = out_ref.shape[2:]
     pieces = rows // STEP
@@ -51,16 +55,8 @@
 
     for k in range(DEPTH):
         arriving(k).start()
-    stored, listed = columns.shape[0], names.shape[1]
-    for a in range(count):
-        for i in range(listed):
-            row = names[a, i]
-            for j in range(listed):
-                column = names[a, j]
-                slot = jnp.int32(-1)
-                for k in range(stored):
-                    slot = jnp.where(columns[k, row] == column, k, slot)
-                slots[(a * listed + i) * listed + j] = slot
+    lists = pltpu.make_async_copy(columns_ref, columns, listing)
+    lists.start()
     for n in range(chunks):
         metric = metric_ref[n * pairs // rows]
         for r in range(pairs):
@@ -79,6 +75,17 @@
             values = part[...].reshape(aux, stride, 128)[:, :pairs]
             made[n % 2, :, :, v * 128 : (v + 1) * 128] = values.astype(BF16)
         leaving(n).start()
+    lists.wait()
+    stored, listed = columns.shape[0], names.shape[1]
+    for a in range(count):
+        for i in range(listed):
+            row = names[a, i]
+            for j in range(listed):
+                column = names[a, j]
+                slot = jnp.int32(-1)
+                for k in range(stored):
+                    slot = jnp.where(columns[k, row] == column, k, slot)
+                slots[(a * listed + i) * listed + j] = slot
     for n in range(chunks - 2, chunks):
         leaving(n).wait()
 
@@ -86,11 +93,11 @@
 def fit(names, columns, metric, raw, window):
     count, aux, merged = raw.shape
     listed = names.shape[1]
-    stride = PAIRS + 8
+    stride = PAIRS + 4
     width = 2 * window
     return pl.pallas_call(
         functools.partial(fit_kernel, PAIRS, stride),
-        in_specs=[in_smem(), in_smem(), in_vmem(), anywhere()],
+        in_specs=[in_smem(), anywhere(), in_vmem(), anywhere()],
         out_specs=[anywhere(), in_smem()],
         out_shape=[
             jax.ShapeDtypeStruct((count, aux, window // 2, width), BF16),
@@ -101,6 +108,8 @@
             pltpu.VMEM((2, aux, PAIRS, width), BF16),
             pltpu.SemaphoreType.DMA((DEPTH,)),
             pltpu.SemaphoreType.DMA((2,)),
+            pltpu.SMEM(columns.shape, jnp.int32),
+            pltpu.SemaphoreType.DMA,
         ]
         + [pltpu.VMEM((aux * stride, 128), F32)] * (width // 128),
         compiler_params=pltpu.CompilerParams(vmem_limit_bytes=VMEM_LIMIT),
@@ -113,11 +122,16 @@
     )(names, columns, metric, raw)
 
 
-def pack_kernel(rows, own_ref, before_ref, after_ref, out_ref, near):
+def pack_kernel(rows_ref, own_ref, before_ref, after_ref, out_ref, near, rows, sems):
     slab = own_ref.shape[0]
+    lists = pltpu.make_async_copy(rows_ref, rows, sems.at[0])
+    blocks = pltpu.make_async_copy(own_ref, near.at[pl.ds(HALO, slab)], sems.at[1])
+    lists.start()
+    blocks.start()
     near[:HALO] = before_ref[...]
-    near[HALO : HALO + slab] = own_ref[...]
     near[HALO + slab :] = after_ref[...]
+    lists.wait()
+    blocks.wait()
     peers, listed = out_ref.shape[:2]
     for peer in range(peers):
         for i in range(listed):
@@ -130,16 +144,20 @@
     peers, _, listed = rows.shape
     return pl.pallas_call(
         pack_kernel,
-        in_specs=[in_smem(), in_vmem(), in_vmem(), in_vmem()],
+        in_specs=[anywhere(), anywhere(), in_vmem(), in_vmem()],
         out_specs=in_vmem(),
-        scratch_shapes=[pltpu.VMEM((slab + 2 * HALO, ob, ob), BF16)],
+        scratch_shapes=[
+            pltpu.VMEM((slab + 2 * HALO, ob, ob), BF16),
+            pltpu.SMEM(rows.shape, jnp.int32),
+            pltpu.SemaphoreType.DMA((2,)),
+        ],
         out_shape=jax.ShapeDtypeStruct((peers, listed, ob, 2 * ob), BF16),
         cost_estimate=pl.CostEstimate(flops=0, bytes_accessed=2**20, transcendentals=0),
         name="pack",
-    )(rows, own, before, after)
-
-
-def mix_kernel(slots, fit_ref, recv_ref, out_ref, dens, held, sems):
+    )(rows, own, held_in_vmem(before), held_in_vmem(after))
+
+
+def mix_kernel(slots_ref, fit_ref, recv_ref, out_ref, dens, held, slots, sems, listing):
     count, aux, pairs, width = fit_ref.shape
     listed, ob = recv_ref.shape[1:3]
     window = width // 2
@@ -149,6 +167,8 @@
         at = (n * PIECE // aux, pl.ds(n * PIECE % aux, PIECE))
         return pltpu.make_async_copy(fit_ref.at[at], held.at[at], sems.at[n])
 
+    lists = pltpu.make_async_copy(slots_ref, slots, listing)
+    lists.start()
     for n in range(DEPTH):
         arriving(n).start()
     out_ref[...] = jnp.zeros_like(out_ref)
@@ -156,6 +176,7 @@
     column = lax.broadcasted_iota(jnp.int32, (window, window), 1)
     turn = (lax.rem(row, 2) * pairs + lax.div(row, 2) == column).astype(BF16)
     across = (((1,), (1,)), ((), ()))
+    lists.wait()
     for a in range(count):
         for i in range(listed):
             blocks = []
@@ -204,12 +225,14 @@
     window = width // 2
     return pl.pallas_call(
         mix_kernel,
-        in_specs=[in_smem(), anywhere(), in_vmem()],
+        in_specs=[anywhere(), anywhere(), in_vmem()],
         out_specs=in_vmem(),
         scratch_shapes=[
             pltpu.VMEM((count, window, window), BF16),
             pltpu.VMEM(fitted.shape, BF16),
+            pltpu.SMEM(slots.shape, jnp.int32),
             pltpu.SemaphoreType.DMA((count * aux // PIECE,)),
+            pltpu.SemaphoreType.DMA,
         ],
         out_shape=jax.ShapeDtypeStruct(received.shape, BF16),
         compiler_params=pltpu.CompilerParams(vmem_limit_bytes=VMEM_LIMIT),
@@ -219,7 +242,7 @@
             transcendentals=0,
         ),
         name="mix",
-    )(slots, fitted, received)
+    )(slots, fitted, held_in_vmem(received))
 
 
 def halves(pair):
@@ -262,7 +285,7 @@
         out_shape=[shape, shape],
         cost_estimate=pl.CostEstimate(flops=0, bytes_accessed=2**19, transcendentals=0),
         name="halo_sums",
-    )(rows, terms)
+    )(rows, held_in_vmem(terms))
 
 
 def own_kernel(rows, terms_ref, own_ref, edge_ref, total):
@@ -293,7 +316,7 @@
         ],
         cost_estimate=pl.CostEstimate(flops=0, bytes_accessed=2**21, transcendentals=0),
         name="own_sums",
-    )(rows, terms)
+    )(rows, held_in_vmem(terms))
 
 
 def edge_kernel(own_ref, edge_ref, before_ref, after_ref, out_ref, rows, sems):
@@ -322,7 +345,7 @@
         scratch_shapes=[pltpu.VMEM(edges.shape, F32), pltpu.SemaphoreType.DMA((2,))],
         input_output_aliases={0: 0},
         name="add_edges",
-    )(own, edges, before, after)
+    )(own, held_in_vmem(edges), held_in_vmem(before), held_in_vmem(after))
 
 
 def ring(value, axis, steps):

time: 82.4 us -> 77.4 us (0.939)
  Pallas kernels: 32.3 us -> 28.3 us
  local copies, waits for them, and re-layouts: 4.16 us -> 3.11 us
    pallas_call x1, Pallas kernels: 11.1 us -> 9.69 us  [fit(): pl.pallas_call(functools.partial(fit_kernel, PAIRS, stride), in_specs=[in...]
    pallas_call x2, Pallas kernels: 14.4 us -> 13.2 us  [the longest x1 11.2 us: mix(): pl.pallas_call(mix_kernel, in_specs=[anywhere(), anywhere(), in_vmem()],...]
    unnamed x10 -> x2, local copies, waits for them, and re-layouts: 2.01 us -> 0.95 us
    pallas_call x1, Pallas kernels: 1.79 us -> 0.8 us  [add_edges(): pl.pallas_call(edge_kernel, in_specs=[pl.BlockSpec(memory_space=pl.ANY),...]
  transfers between devices with their start and end apart: 6 -> 6, of which waited for: 3 -> 3; matrix products, arithmetic and copies ran while one was open for 2% -> 2% of each run, Pallas kernels for 17% -> 16%
where the time goes in v3:
time: 77.4 us; the launch traced here: 76.8 us
  Pallas kernels  28.3 us (37%)
  starting transfers between devices  23.9 us (31%)
  blocking collectives  15.5 us (20%)
  waiting for transfers between devices  5.19 us (7%)
  local copies, waits for them, and re-layouts  3.11 us (4%)
    all_to_all x1, blocking collectives, per_device(): terms = lax.all_to_all(terms, 'dev', 0, 0, tiled=True)  15.5 us
    pallas_call x1, Pallas kernels, mix(): pl.pallas_call(mix_kernel, in_specs=[anywhere(), anywhere(), in_vmem()],...  11.2 us
    pallas_call x1, Pallas kernels, fit(): pl.pallas_call(functools.partial(fit_kernel, PAIRS, stride), in_specs=[in...  9.69 us
    ppermute x4, starting transfers between devices, ring(): return lax.ppermute(value, axis, pairs)  8.7 us
    all_to_all x1, starting transfers between devices, per_device(): received = lax.all_to_all(packed, 'dev', 0, 0, tiled=True)  7.82 us
    all_to_all x1, starting transfers between devices, per_device(): names = lax.all_to_all(names, 'dev', 0, 0, tiled=True)  7.38 us
    ppermute x4, waiting for transfers between devices, ring(): return lax.ppermute(value, axis, pairs)  4.68 us
    pallas_call x1, Pallas kernels, own_sums(): pl.pallas_call(own_kernel, in_specs=[in_smem(), in_vmem()], out_specs=[in...  2.49 us
  transfers between devices with their start and end apart: 6, of which 3 were waited for; matrix products, arithmetic and copies ran while one was open for 2% of the time, Pallas kernels for 16%

profile of v3, /device:TPU:8, one launch (start us, length us, event | category | flops | bytes accessed | tf_op | source)
XLA Modules:
  0.0 76.8 jit_solution(7054957977355485289)
XLA Ops:
  0.0 1.3 %broadcast_in_dim.2 = s32[8,2,3]{2,1,0:T(2,128)} broadcast(s32[2,3]{1,0:T(2,128)} %names.1), dimensions={1,2} | broadcast | bytes 216 | tf_op jit(solution)/shard_map/broadcast_in_dim | solution.py:365
  1.3 7.4 %all-to-all-start = ((s32[8,2,3]{2,1,0:T(2,128)}), s32[8,2,3]{2,1,0:T(2,128)S(1)}, u32[]{:S(2)}, u32[]{:S(2)}) async-start(s32[8,2,3]{2,1,0:T(2,128)} %broadcast_in_dim.2), calls=%async_computation | async-start | bytes 16384 | tf_op jit(solution)/shard_map/all_to_all | solution.py:366
  8.7 0.9 %slice_bitcast_fusion = (bf16[4,64,64]{2,1,0:T(8,128)(2,1)S(1)}, bf16[4,64,64]{2,1,0:T(8,128)(2,1)S(1)}) fusion(bf16[32,1,64,64]{3,2,0,1:T(8,128)(2,1)} %bitcast.10), kind=kLoop, calls=%fused_computation | loop fusion | bytes 131072 | tf_op jit(solution)/shard_map/slice | solution.py:370
  9.5 4.8 %collective-permute-start.1 = (bf16[4,64,64]{2,1,0:T(8,128)(2,1)S(1)}, bf16[4,64,64]{2,1,0:T(8,128)(2,1)S(1)}, u32[]{:S(2)}, u32[]{:S(2)}) collective-permute-start(bf16[4,64,64]{2,1,0:T(8,128)(2,1)S(1)} %get-tuple-element.17), channel_id=1, source_target_pairs={{0,248},{8,0},{16,8},{24,16},{32,24},{40,32},{48,40},{56,48},{64,5... | collective-permute-start | bytes 98312 | tf_op jit(solution)/shard_map/ppermute | solution.py:354
  14.4 0.0 collective-permute-start
  14.4 0.5 all-to-all-done
  14.9 0.6 and_select_fusion.rows_ref.rows
  15.5 0.8 %collective-permute-done.1.after_ref = bf16[4,64,64]{2,1,0:T(8,128)(2,1)S(1)} collective-permute-done((bf16[4,64,64]{2,1,0:T(8,128)(2,1)S(1)}, bf16[4,64,64]{2,1,0:T(8,128)(2,1)S(1)}, u32[]{:S(2)}, u32[]{:S(2)}) %collective-permute-start.1) | collective-permute-done | bytes 32800 | tf_op jit(solution)/shard_map/ppermute | solution.py:354
  16.3 3.9 %collective-permute-done.before_ref = bf16[4,64,64]{2,1,0:T(8,128)(2,1)S(1)} collective-permute-done((bf16[4,64,64]{2,1,0:T(8,128)(2,1)S(1)}, bf16[4,64,64]{2,1,0:T(8,128)(2,1)S(1)}, u32[]{:S(2)}, u32[]{:S(2)}) %collective-permute-start) | collective-permute-done | bytes 32800 | tf_op jit(solution)/shard_map/ppermute | solution.py:354
  20.2 2.0 %pack.1 = bf16[8,3,64,128]{3,2,1,0:T(8,128)(2,1)} custom-call(s32[8,2,3]{2,1,0:T(2,128)} %and_select_fusion.rows_ref.rows, bf16[32,64,64]{2,1,0:T(8,128)(2,1)} %bitcast.11, bf16[4,64,64]{2,1,0:T(8,128)(2,1)S(1)} %collective-permute-done.before_ref, bf16[4,64,64]{2,1,0:T(8,128)(2,1)S(1)} %collective-permute-done.1.after_ref), custom_call_target="tpu_custom_call" | custom-call | bytes 1048576 | tf_op jit(solution)/shard_map/pack/pallas_call | solution.py:145
  22.2 7.8 %all-to-all-start.1 = ((bf16[8,3,64,128]{3,2,1,0:T(8,128)(2,1)}), bf16[8,3,64,128]{3,2,1,0:T(8,128)(2,1)S(1)}, u32[]{:S(2)}, u32[]{:S(2)}) async-start(bf16[8,3,64,128]{3,2,1,0:T(8,128)(2,1)} %pack.1), calls=%async_computation.1 | async-start | bytes 786432 | tf_op jit(solution)/shard_map/all_to_all | solution.py:373
  30.0 9.7 %fit.1 = (bf16[2,64,96,384]{3,2,1,0:T(8,128)(2,1)}, s32[18]{0:T(128)}) custom-call(s32[2,3]{1,0:T(2,128)} %names.1, s32[8,1024]{1,0:T(8,128)} %bitcast.12, bf16[2,64,64]{2,1,0:T(8,128)(2,1)} %metric_ref.1, bf16[2,64,36864]{2,1,0:T(8,128)(2,1)} %raw_ref.1), custom_call_target="tpu_custom_call" | custom-call | flops 603979776 | bytes 18874368 | tf_op jit(solution)/shard_map/fit/pallas_call | solution.py:98
  39.7 0.0 all-to-all-done.1.recv_ref
  39.7 11.2 %mix.1 = bf16[8,3,64,128]{3,2,1,0:T(8,128)(2,1)} custom-call(s32[18]{0:T(128)} %get-tuple-element.11.slots_ref, bf16[2,64,96,384]{3,2,1,0:T(8,128)(2,1)} %get-tuple-element.12.fit_ref, bf16[8,3,64,128]{3,2,1,0:T(8,128)(2,1)S(1)} %all-to-all-done.1.recv_ref), custom_call_target="tpu_custom_call" | custom-call | flops 3623878656 | bytes 9437184 | tf_op jit(solution)/shard_map/mix/pallas_call | solution.py:226
  50.9 15.5 %all_to_all.15.terms_ref = bf16[8,3,64,128]{3,2,1,0:T(8,128)(2,1)S(1)} all-to-all(bf16[8,3,64,128]{3,2,1,0:T(8,128)(2,1)} %mix.1), channel_id=1, replica_groups=mesh['ta'=32,'dev'=8] {'dev'}, dimensions={0} | all-to-all | bytes 786432 | tf_op jit(solution)/shard_map/all_to_all | solution.py:376
  66.4 2.1 %halo_sums.1 = (f32[2,64,128]{2,1,0:T(8,128)}, f32[2,64,128]{2,1,0:T(8,128)}) custom-call(s32[8,2,3]{2,1,0:T(2,128)} %and_select_fusion.rows_ref.rows, bf16[8,3,64,128]{3,2,1,0:T(8,128)(2,1)S(1)} %all_to_all.15.terms_ref), custom_call_target="tpu_custom_call" | custom-call | bytes 524288 | tf_op jit(solution)/shard_map/halo_sums/pallas_call | solution.py:280
  68.5 0.0 collective-permute-start.2
  68.5 3.9 %collective-permute-start.3 = (f32[2,64,128]{2,1,0:T(8,128)}, f32[2,64,128]{2,1,0:T(8,128)S(1)}, u32[]{:S(2)}, u32[]{:S(2)}) collective-permute-start(f32[2,64,128]{2,1,0:T(8,128)} %get-tuple-element.16), channel_id=1, source_target_pairs={{0,248},{8,0},{16,8},{24,16},{32,24},{40,32},{48,40},{56,48},{64,5... | collective-permute-start | bytes 196616 | tf_op jit(solution)/shard_map/ppermute | solution.py:354
  72.4 2.5 %own_sums.1 = (f32[32,64,64]{2,1,0:T(8,128)}, f32[8,64,64]{2,1,0:T(8,128)}) custom-call(s32[8,2,3]{2,1,0:T(2,128)} %and_select_fusion.rows_ref.rows, bf16[8,3,64,128]{3,2,1,0:T(8,128)(2,1)S(1)} %all_to_all.15.terms_ref), custom_call_target="tpu_custom_call" | custom-call | bytes 2097152 | tf_op jit(solution)/shard_map/own_sums/pallas_call | solution.py:308
  74.8 0.0 collective-permute-done.2.before_ref
  74.8 0.0 collective-permute-done.3.after_ref
  74.9 0.0 copy-start
  74.9 0.9 %copy-done = f32[8,64,64]{2,1,0:T(8,128)S(1)} copy-done((f32[8,64,64]{2,1,0:T(8,128)S(1)}, f32[8,64,64]{2,1,0:T(8,128)}, u32[]{:S(2)}) %copy-start) | copy-done | bytes 131096
  75.8 0.8 %add_edges.1 = f32[32,64,64]{2,1,0:T(8,128)} custom-call(f32[32,64,64]{2,1,0:T(8,128)} %get-tuple-element.13.own_ref, f32[8,64,64]{2,1,0:T(8,128)S(1)} %copy-done, f32[2,64,128]{2,1,0:T(8,128)S(1)} %collective-permute-done.2.before_ref, f32[2,64,128]{2,1,0:T(8,128)S(1)} %collective-permute-done.3.after_ref), custom_call_target="tpu_custom_call", output_to_operand_aliasing={{}: (0, {})} | custom-call | tf_op jit(solution)/shard_map/add_edges/pallas_call | solution.py:340
Async XLA Ops:
  1.3 13.6 %all-to-all-start = ((s32[8,2,3]{2,1,0:T(2,128)}), s32[8,2,3]{2,1,0:T(2,128)S(1)}, u32[]{:S(2)}, u32[]{:S(2)}) async-start(s32[8,2,3]{2,1,0:T(2,128)} %broadcast_in_dim.2), calls=%async_computation | async-start | bytes 16384 | tf_op jit(solution)/shard_map/all_to_all | solution.py:366
  9.5 6.7 %collective-permute-start.1 = (bf16[4,64,64]{2,1,0:T(8,128)(2,1)S(1)}, bf16[4,64,64]{2,1,0:T(8,128)(2,1)S(1)}, u32[]{:S(2)}, u32[]{:S(2)}) collective-permute-start(bf16[4,64,64]{2,1,0:T(8,128)(2,1)S(1)} %get-tuple-element.17), channel_id=1, source_target_pairs={{0,248},{8,0},{16,8},{24,16},{32,24},{40,32},{48,40},{56,48},{64,5... | collective-permute-start | bytes 98312 | tf_op jit(solution)/shard_map/ppermute | solution.py:354
  14.4 5.8 %collective-permute-start = (bf16[4,64,64]{2,1,0:T(8,128)(2,1)S(1)}, bf16[4,64,64]{2,1,0:T(8,128)(2,1)S(1)}, u32[]{:S(2)}, u32[]{:S(2)}) collective-permute-start(bf16[4,64,64]{2,1,0:T(8,128)(2,1)S(1)} %get-tuple-element.18), channel_id=1, source_target_pairs={{0,8},{8,16},{16,24},{24,32},{32,40},{40,48},{48,56},{56,64},{64,7... | collective-permute-start | bytes 98312 | tf_op jit(solution)/shard_map/ppermute | solution.py:354
  22.2 17.5 %all-to-all-start.1 = ((bf16[8,3,64,128]{3,2,1,0:T(8,128)(2,1)}), bf16[8,3,64,128]{3,2,1,0:T(8,128)(2,1)S(1)}, u32[]{:S(2)}, u32[]{:S(2)}) async-start(bf16[8,3,64,128]{3,2,1,0:T(8,128)(2,1)} %pack.1), calls=%async_computation.1 | async-start | bytes 786432 | tf_op jit(solution)/shard_map/all_to_all | solution.py:373
  68.5 6.3 %collective-permute-start.2 = (f32[2,64,128]{2,1,0:T(8,128)}, f32[2,64,128]{2,1,0:T(8,128)S(1)}, u32[]{:S(2)}, u32[]{:S(2)}) collective-permute-start(f32[2,64,128]{2,1,0:T(8,128)} %get-tuple-element.15), channel_id=1, source_target_pairs={{0,8},{8,16},{16,24},{24,32},{32,40},{40,48},{48,56},{56,64},{64,7... | collective-permute-start | bytes 196616 | tf_op jit(solution)/shard_map/ppermute | solution.py:354
  68.5 6.3 %collective-permute-start.3 = (f32[2,64,128]{2,1,0:T(8,128)}, f32[2,64,128]{2,1,0:T(8,128)S(1)}, u32[]{:S(2)}, u32[]{:S(2)}) collective-permute-start(f32[2,64,128]{2,1,0:T(8,128)} %get-tuple-element.16), channel_id=1, source_target_pairs={{0,248},{8,0},{16,8},{24,16},{32,24},{40,32},{48,40},{56,48},{64,5... | collective-permute-start | bytes 196616 | tf_op jit(solution)/shard_map/ppermute | solution.py:354
  74.9 1.0 %copy-start = (f32[8,64,64]{2,1,0:T(8,128)S(1)}, f32[8,64,64]{2,1,0:T(8,128)}, u32[]{:S(2)}) copy-start(f32[8,64,64]{2,1,0:T(8,128)} %get-tuple-element.14.edge_ref) | copy-start | bytes 393220

commit v4 on v3

--- a/solution.py
+++ b/solution.py
@@ -14,6 +14,7 @@
 STEP = 32
 DEPTH = 3
 PIECE = 16
+MDEPTH = 8
 PARTS = ((16, 16, 32), (32, 32))
 VMEM_LIMIT = 56 * 2**20
 
@@ -157,7 +158,7 @@
     )(rows, own, held_in_vmem(before), held_in_vmem(after))
 
 
-def mix_kernel(slots_ref, fit_ref, recv_ref, out_ref, dens, held, slots, sems, listing):
+def mix_kernel(slots_ref, fit_ref, recv_ref, out_ref, dens, made, held, slots, sems, listing):
     count, aux, pairs, width = fit_ref.shape
     listed, ob = recv_ref.shape[1:3]
     window = width // 2
@@ -169,14 +170,15 @@
 
     lists = pltpu.make_async_copy(slots_ref, slots, listing)
     lists.start()
-    for n in range(DEPTH):
+    for n in range(MDEPTH):
         arriving(n).start()
-    out_ref[...] = jnp.zeros_like(out_ref)
+    made[...] = jnp.zeros_like(made)
     row = lax.broadcasted_iota(jnp.int32, (window, window), 0)
     column = lax.broadcasted_iota(jnp.int32, (window, window), 1)
-    turn = (lax.rem(row, 2) * pairs + lax.div(row, 2) == column).astype(BF16)
+    turn = ((row & 1) * pairs + (row >> 1) == column).astype(BF16)
     across = (((1,), (1,)), ((), ()))
     lists.wait()
+    sums = []
     for a in range(count):
         for i in range(listed):
             blocks = []
@@ -192,8 +194,8 @@
         for part in PARTS[a]:
             for n in range((a * aux + done) // PIECE, (a * aux + done + part) // PIECE):
                 arriving(n).wait()
-                if n + DEPTH < total:
-                    arriving(n + DEPTH).start()
+                if n + MDEPTH < total:
+                    arriving(n + MDEPTH).start()
             rows = held[a, pl.ds(done, part)]
             fitted = jnp.concatenate([rows[..., :window], rows[..., window:]], axis=1)
             fitted = fitted.reshape(part * window, window)
@@ -206,18 +208,18 @@
                 summed = term if summed is None else summed + term
             done += part
 
-        half = lax.dot_general(
-            summed.astype(BF16), turn, across, preferred_element_type=F32
-        ).astype(BF16)
-        terms = jnp.dot(turn, half, preferred_element_type=F32).astype(BF16)
+        sums.append(summed.astype(BF16))
+
+    halfs = [lax.dot_general(x, turn, across, preferred_element_type=F32).astype(BF16) for x in sums]
+    terms = [jnp.dot(turn, x, preferred_element_type=F32).astype(BF16) for x in halfs]
+    for a in range(count):
         for i in range(listed):
             for j in range(listed):
                 slot = slots[(a * listed + i) * listed + j]
-                block = terms[i * ob : (i + 1) * ob, j * ob : (j + 1) * ob]
-
-                @pl.when(slot >= 0)
-                def _():
-                    out_ref[slot, i, :, a * ob : (a + 1) * ob] = block
+                at = jnp.where(slot >= 0, slot, out_ref.shape[0])
+                block = terms[a][i * ob : (i + 1) * ob, j * ob : (j + 1) * ob]
+                made[at, i, :, a * ob : (a + 1) * ob] = block
+    out_ref[...] = made[: out_ref.shape[0]]
 
 
 def mix(slots, fitted, received):
@@ -229,6 +231,7 @@
         out_specs=in_vmem(),
         scratch_shapes=[
             pltpu.VMEM((count, window, window), BF16),
+            pltpu.VMEM((received.shape[0] + 1,) + received.shape[1:], BF16),
             pltpu.VMEM(fitted.shape, BF16),
             pltpu.SMEM(slots.shape, jnp.int32),
             pltpu.SemaphoreType.DMA((count * aux // PIECE,)),
@@ -260,13 +263,11 @@
     total[...] = jnp.zeros_like(total)
     for peer in range(peers):
         for i in range(listed):
+            pair = halves(terms_ref[peer, i].astype(F32))
             for a in range(2):
                 row = rows[peer, a, i]
-
-                @pl.when((row < HALO) | (row >= HALO + slab))
-                def _():
-                    at = jnp.where(row < HALO, row, row - slab)
-                    total[at] += halves(terms_ref[peer, i].astype(F32))[a]
+                other = jnp.where(row < HALO + slab, 2 * HALO + a, row - slab)
+                total[jnp.where(row < HALO, row, other)] += pair[a]
 
     for ref, start in ((low_ref, 0), (high_ref, HALO)):
         sums = folded(total[start : start + HALO])
@@ -281,7 +282,7 @@
         functools.partial(halo_kernel, slab),
         in_specs=[in_smem(), in_vmem()],
         out_specs=[in_vmem(), in_vmem()],
-        scratch_shapes=[pltpu.VMEM((2 * HALO, ob, lanes), F32)],
+        scratch_shapes=[pltpu.VMEM((2 * HALO + 2, ob, lanes), F32)],
         out_shape=[shape, shape],
         cost_estimate=pl.CostEstimate(flops=0, bytes_accessed=2**19, transcendentals=0),
         name="halo_sums",

time: 77.4 us -> 76.5 us (0.988)
  Pallas kernels: 28.3 us -> 27.3 us
where the time goes in v4:
time: 76.5 us; the launch traced here: 75.9 us
  Pallas kernels  27.3 us (36%)
  starting transfers between devices  23.9 us (31%)
  blocking collectives  15.6 us (20%)
  waiting for transfers between devices  5.19 us (7%)
  local copies, waits for them, and re-layouts  3.11 us (4%)
    all_to_all x1, blocking collectives, per_device(): terms = lax.all_to_all(terms, 'dev', 0, 0, tiled=True)  15.6 us
    pallas_call x1, Pallas kernels, mix(): pl.pallas_call(mix_kernel, in_specs=[anywhere(), anywhere(), in_vmem()],...  10.4 us
    pallas_call x1, Pallas kernels, fit(): pl.pallas_call(functools.partial(fit_kernel, PAIRS, stride), in_specs=[in...  9.69 us
    ppermute x4, starting transfers between devices, ring(): return lax.ppermute(value, axis, pairs)  8.7 us
    all_to_all x1, starting transfers between devices, per_device(): received = lax.all_to_all(packed, 'dev', 0, 0, tiled=True)  7.82 us
    all_to_all x1, starting transfers between devices, per_device(): names = lax.all_to_all(names, 'dev', 0, 0, tiled=True)  7.38 us
    ppermute x4, waiting for transfers between devices, ring(): return lax.ppermute(value, axis, pairs)  4.68 us
    pallas_call x1, Pallas kernels, own_sums(): pl.pallas_call(own_kernel, in_specs=[in_smem(), in_vmem()], out_specs=[in...  2.48 us
  transfers between devices with their start and end apart: 6, of which 3 were waited for; matrix products, arithmetic and copies ran while one was open for 2% of the time, Pallas kernels for 16%

profile of v4, /device:TPU:8, one launch (start us, length us, event | category | flops | bytes accessed | tf_op | source)
XLA Modules:
  0.0 75.9 jit_solution(8127181223448665469)
XLA Ops:
  0.0 1.3 %broadcast_in_dim.2 = s32[8,2,3]{2,1,0:T(2,128)} broadcast(s32[2,3]{1,0:T(2,128)} %names.1), dimensions={1,2} | broadcast | bytes 216 | tf_op jit(solution)/shard_map/broadcast_in_dim | solution.py:366
  1.3 7.4 %all-to-all-start = ((s32[8,2,3]{2,1,0:T(2,128)}), s32[8,2,3]{2,1,0:T(2,128)S(1)}, u32[]{:S(2)}, u32[]{:S(2)}) async-start(s32[8,2,3]{2,1,0:T(2,128)} %broadcast_in_dim.2), calls=%async_computation | async-start | bytes 16384 | tf_op jit(solution)/shard_map/all_to_all | solution.py:367
  8.7 0.9 %slice_bitcast_fusion = (bf16[4,64,64]{2,1,0:T(8,128)(2,1)S(1)}, bf16[4,64,64]{2,1,0:T(8,128)(2,1)S(1)}) fusion(bf16[32,1,64,64]{3,2,0,1:T(8,128)(2,1)} %bitcast.10), kind=kLoop, calls=%fused_computation | loop fusion | bytes 131072 | tf_op jit(solution)/shard_map/slice | solution.py:371
  9.5 4.8 %collective-permute-start.1 = (bf16[4,64,64]{2,1,0:T(8,128)(2,1)S(1)}, bf16[4,64,64]{2,1,0:T(8,128)(2,1)S(1)}, u32[]{:S(2)}, u32[]{:S(2)}) collective-permute-start(bf16[4,64,64]{2,1,0:T(8,128)(2,1)S(1)} %get-tuple-element.17), channel_id=1, source_target_pairs={{0,248},{8,0},{16,8},{24,16},{32,24},{40,32},{48,40},{56,48},{64,5... | collective-permute-start | bytes 98312 | tf_op jit(solution)/shard_map/ppermute | solution.py:355
  14.4 0.0 collective-permute-start
  14.4 0.5 all-to-all-done
  14.9 0.6 and_select_fusion.rows_ref.rows
  15.5 0.8 %collective-permute-done.1.after_ref = bf16[4,64,64]{2,1,0:T(8,128)(2,1)S(1)} collective-permute-done((bf16[4,64,64]{2,1,0:T(8,128)(2,1)S(1)}, bf16[4,64,64]{2,1,0:T(8,128)(2,1)S(1)}, u32[]{:S(2)}, u32[]{:S(2)}) %collective-permute-start.1) | collective-permute-done | bytes 32800 | tf_op jit(solution)/shard_map/ppermute | solution.py:355
  16.3 3.9 %collective-permute-done.before_ref = bf16[4,64,64]{2,1,0:T(8,128)(2,1)S(1)} collective-permute-done((bf16[4,64,64]{2,1,0:T(8,128)(2,1)S(1)}, bf16[4,64,64]{2,1,0:T(8,128)(2,1)S(1)}, u32[]{:S(2)}, u32[]{:S(2)}) %collective-permute-start) | collective-permute-done | bytes 32800 | tf_op jit(solution)/shard_map/ppermute | solution.py:355
  20.2 2.0 %pack.1 = bf16[8,3,64,128]{3,2,1,0:T(8,128)(2,1)} custom-call(s32[8,2,3]{2,1,0:T(2,128)} %and_select_fusion.rows_ref.rows, bf16[32,64,64]{2,1,0:T(8,128)(2,1)} %bitcast.11, bf16[4,64,64]{2,1,0:T(8,128)(2,1)S(1)} %collective-permute-done.before_ref, bf16[4,64,64]{2,1,0:T(8,128)(2,1)S(1)} %collective-permute-done.1.after_ref), custom_call_target="tpu_custom_call" | custom-call | bytes 1048576 | tf_op jit(solution)/shard_map/pack/pallas_call | solution.py:146
  22.2 7.8 %all-to-all-start.1 = ((bf16[8,3,64,128]{3,2,1,0:T(8,128)(2,1)}), bf16[8,3,64,128]{3,2,1,0:T(8,128)(2,1)S(1)}, u32[]{:S(2)}, u32[]{:S(2)}) async-start(bf16[8,3,64,128]{3,2,1,0:T(8,128)(2,1)} %pack.1), calls=%async_computation.1 | async-start | bytes 786432 | tf_op jit(solution)/shard_map/all_to_all | solution.py:374
  30.0 9.7 %fit.1 = (bf16[2,64,96,384]{3,2,1,0:T(8,128)(2,1)}, s32[18]{0:T(128)}) custom-call(s32[2,3]{1,0:T(2,128)} %names.1, s32[8,1024]{1,0:T(8,128)} %bitcast.12, bf16[2,64,64]{2,1,0:T(8,128)(2,1)} %metric_ref.1, bf16[2,64,36864]{2,1,0:T(8,128)(2,1)} %raw_ref.1), custom_call_target="tpu_custom_call" | custom-call | flops 603979776 | bytes 18874368 | tf_op jit(solution)/shard_map/fit/pallas_call | solution.py:99
  39.7 0.0 all-to-all-done.1.recv_ref
  39.7 10.4 %mix.1 = bf16[8,3,64,128]{3,2,1,0:T(8,128)(2,1)} custom-call(s32[18]{0:T(128)} %get-tuple-element.11.slots_ref, bf16[2,64,96,384]{3,2,1,0:T(8,128)(2,1)} %get-tuple-element.12.fit_ref, bf16[8,3,64,128]{3,2,1,0:T(8,128)(2,1)S(1)} %all-to-all-done.1.recv_ref), custom_call_target="tpu_custom_call" | custom-call | flops 3623878656 | bytes 9437184 | tf_op jit(solution)/shard_map/mix/pallas_call | solution.py:228
  50.1 15.6 %all_to_all.15.terms_ref = bf16[8,3,64,128]{3,2,1,0:T(8,128)(2,1)S(1)} all-to-all(bf16[8,3,64,128]{3,2,1,0:T(8,128)(2,1)} %mix.1), channel_id=1, replica_groups=mesh['ta'=32,'dev'=8] {'dev'}, dimensions={0} | all-to-all | bytes 786432 | tf_op jit(solution)/shard_map/all_to_all | solution.py:377
  65.8 1.9 %halo_sums.1 = (f32[2,64,128]{2,1,0:T(8,128)}, f32[2,64,128]{2,1,0:T(8,128)}) custom-call(s32[8,2,3]{2,1,0:T(2,128)} %and_select_fusion.rows_ref.rows, bf16[8,3,64,128]{3,2,1,0:T(8,128)(2,1)S(1)} %all_to_all.15.terms_ref), custom_call_target="tpu_custom_call" | custom-call | bytes 524288 | tf_op jit(solution)/shard_map/halo_sums/pallas_call | solution.py:281
  67.7 0.0 collective-permute-start.2
  67.7 3.9 %collective-permute-start.3 = (f32[2,64,128]{2,1,0:T(8,128)}, f32[2,64,128]{2,1,0:T(8,128)S(1)}, u32[]{:S(2)}, u32[]{:S(2)}) collective-permute-start(f32[2,64,128]{2,1,0:T(8,128)} %get-tuple-element.16), channel_id=1, source_target_pairs={{0,248},{8,0},{16,8},{24,16},{32,24},{40,32},{48,40},{56,48},{64,5... | collective-permute-start | bytes 196616 | tf_op jit(solution)/shard_map/ppermute | solution.py:355
  71.5 2.5 %own_sums.1 = (f32[32,64,64]{2,1,0:T(8,128)}, f32[8,64,64]{2,1,0:T(8,128)}) custom-call(s32[8,2,3]{2,1,0:T(2,128)} %and_select_fusion.rows_ref.rows, bf16[8,3,64,128]{3,2,1,0:T(8,128)(2,1)S(1)} %all_to_all.15.terms_ref), custom_call_target="tpu_custom_call" | custom-call | bytes 2097152 | tf_op jit(solution)/shard_map/own_sums/pallas_call | solution.py:309
  74.0 0.0 collective-permute-done.2.before_ref
  74.0 0.0 collective-permute-done.3.after_ref
  74.0 0.0 copy-start
  74.0 0.9 %copy-done = f32[8,64,64]{2,1,0:T(8,128)S(1)} copy-done((f32[8,64,64]{2,1,0:T(8,128)S(1)}, f32[8,64,64]{2,1,0:T(8,128)}, u32[]{:S(2)}) %copy-start) | copy-done | bytes 131096
  75.0 0.8 %add_edges.1 = f32[32,64,64]{2,1,0:T(8,128)} custom-call(f32[32,64,64]{2,1,0:T(8,128)} %get-tuple-element.13.own_ref, f32[8,64,64]{2,1,0:T(8,128)S(1)} %copy-done, f32[2,64,128]{2,1,0:T(8,128)S(1)} %collective-permute-done.2.before_ref, f32[2,64,128]{2,1,0:T(8,128)S(1)} %collective-permute-done.3.after_ref), custom_call_target="tpu_custom_call", output_to_operand_aliasing={{}: (0, {})} | custom-call | tf_op jit(solution)/shard_map/add_edges/pallas_call | solution.py:341
Async XLA Ops:
  1.3 13.6 %all-to-all-start = ((s32[8,2,3]{2,1,0:T(2,128)}), s32[8,2,3]{2,1,0:T(2,128)S(1)}, u32[]{:S(2)}, u32[]{:S(2)}) async-start(s32[8,2,3]{2,1,0:T(2,128)} %broadcast_in_dim.2), calls=%async_computation | async-start | bytes 16384 | tf_op jit(solution)/shard_map/all_to_all | solution.py:367
  9.5 6.7 %collective-permute-start.1 = (bf16[4,64,64]{2,1,0:T(8,128)(2,1)S(1)}, bf16[4,64,64]{2,1,0:T(8,128)(2,1)S(1)}, u32[]{:S(2)}, u32[]{:S(2)}) collective-permute-start(bf16[4,64,64]{2,1,0:T(8,128)(2,1)S(1)} %get-tuple-element.17), channel_id=1, source_target_pairs={{0,248},{8,0},{16,8},{24,16},{32,24},{40,32},{48,40},{56,48},{64,5... | collective-permute-start | bytes 98312 | tf_op jit(solution)/shard_map/ppermute | solution.py:355
  14.4 5.8 %collective-permute-start = (bf16[4,64,64]{2,1,0:T(8,128)(2,1)S(1)}, bf16[4,64,64]{2,1,0:T(8,128)(2,1)S(1)}, u32[]{:S(2)}, u32[]{:S(2)}) collective-permute-start(bf16[4,64,64]{2,1,0:T(8,128)(2,1)S(1)} %get-tuple-element.18), channel_id=1, source_target_pairs={{0,8},{8,16},{16,24},{24,32},{32,40},{40,48},{48,56},{56,64},{64,7... | collective-permute-start | bytes 98312 | tf_op jit(solution)/shard_map/ppermute | solution.py:355
  22.2 17.5 %all-to-all-start.1 = ((bf16[8,3,64,128]{3,2,1,0:T(8,128)(2,1)}), bf16[8,3,64,128]{3,2,1,0:T(8,128)(2,1)S(1)}, u32[]{:S(2)}, u32[]{:S(2)}) async-start(bf16[8,3,64,128]{3,2,1,0:T(8,128)(2,1)} %pack.1), calls=%async_computation.1 | async-start | bytes 786432 | tf_op jit(solution)/shard_map/all_to_all | solution.py:374
  67.7 6.3 %collective-permute-start.2 = (f32[2,64,128]{2,1,0:T(8,128)}, f32[2,64,128]{2,1,0:T(8,128)S(1)}, u32[]{:S(2)}, u32[]{:S(2)}) collective-permute-start(f32[2,64,128]{2,1,0:T(8,128)} %get-tuple-element.15), channel_id=1, source_target_pairs={{0,8},{8,16},{16,24},{24,32},{32,40},{40,48},{48,56},{56,64},{64,7... | collective-permute-start | bytes 196616 | tf_op jit(solution)/shard_map/ppermute | solution.py:355
  67.7 6.3 %collective-permute-start.3 = (f32[2,64,128]{2,1,0:T(8,128)}, f32[2,64,128]{2,1,0:T(8,128)S(1)}, u32[]{:S(2)}, u32[]{:S(2)}) collective-permute-start(f32[2,64,128]{2,1,0:T(8,128)} %get-tuple-element.16), channel_id=1, source_target_pairs={{0,248},{8,0},{16,8},{24,16},{32,24},{40,32},{48,40},{56,48},{64,5... | collective-permute-start | bytes 196616 | tf_op jit(solution)/shard_map/ppermute | solution.py:355
  74.0 1.0 %copy-start = (f32[8,64,64]{2,1,0:T(8,128)S(1)}, f32[8,64,64]{2,1,0:T(8,128)}, u32[]{:S(2)}) copy-start(f32[8,64,64]{2,1,0:T(8,128)} %get-tuple-element.14.edge_ref) | copy-start | bytes 393220

commit v5 on v4

--- a/solution.py
+++ b/solution.py
@@ -73,7 +73,7 @@
         if n >= 2:
             leaving(n - 2).wait()
         for v, part in enumerate(parts):
-            values = part[...].reshape(aux, stride, 128)[:, :pairs]
+            values = part[: aux * stride].reshape(aux, stride, 128)[:, :pairs]
             made[n % 2, :, :, v * 128 : (v + 1) * 128] = values.astype(BF16)
         leaving(n).start()
     lists.wait()
@@ -112,7 +112,7 @@
             pltpu.SMEM(columns.shape, jnp.int32),
             pltpu.SemaphoreType.DMA,
         ]
-        + [pltpu.VMEM((aux * stride, 128), F32)] * (width // 128),
+        + [pltpu.VMEM(((aux + 1) * stride, 128), F32)] * (width // 128),
         compiler_params=pltpu.CompilerParams(vmem_limit_bytes=VMEM_LIMIT),
         cost_estimate=pl.CostEstimate(
             flops=2 * count * aux * aux * merged,

time: 76.5 us -> 76.6 us (level)
  no operation moved by 1% of the time
where the time goes in v5:
time: 76.6 us; the launch traced here: 76 us
  Pallas kernels  27.4 us (36%)
  starting transfers between devices  23.9 us (31%)
  blocking collectives  15.6 us (20%)
  waiting for transfers between devices  5.19 us (7%)
  local copies, waits for them, and re-layouts  3.11 us (4%)
    all_to_all x1, blocking collectives, per_device(): terms = lax.all_to_all(terms, 'dev', 0, 0, tiled=True)  15.6 us
    pallas_call x1, Pallas kernels, mix(): pl.pallas_call(mix_kernel, in_specs=[anywhere(), anywhere(), in_vmem()],...  10.4 us
    pallas_call x1, Pallas kernels, fit(): pl.pallas_call(functools.partial(fit_kernel, PAIRS, stride), in_specs=[in...  9.75 us
    ppermute x4, starting transfers between devices, ring(): return lax.ppermute(value, axis, pairs)  8.7 us
    all_to_all x1, starting transfers between devices, per_device(): received = lax.all_to_all(packed, 'dev', 0, 0, tiled=True)  7.82 us
    all_to_all x1, starting transfers between devices, per_device(): names = lax.all_to_all(names, 'dev', 0, 0, tiled=True)  7.38 us
    ppermute x4, waiting for transfers between devices, ring(): return lax.ppermute(value, axis, pairs)  4.68 us
    pallas_call x1, Pallas kernels, own_sums(): pl.pallas_call(own_kernel, in_specs=[in_smem(), in_vmem()], out_specs=[in...  2.49 us
  transfers between devices with their start and end apart: 6, of which 3 were waited for; matrix products, arithmetic and copies ran while one was open for 2% of the time, Pallas kernels for 16%

profile of v5, /device:TPU:8, one launch (start us, length us, event | category | flops | bytes accessed | tf_op | source)
XLA Modules:
  0.0 76.0 jit_solution(10628753896310471624)
XLA Ops:
  0.0 1.3 %broadcast_in_dim.2 = s32[8,2,3]{2,1,0:T(2,128)} broadcast(s32[2,3]{1,0:T(2,128)} %names.1), dimensions={1,2} | broadcast | bytes 216 | tf_op jit(solution)/shard_map/broadcast_in_dim | solution.py:366
  1.3 7.4 %all-to-all-start = ((s32[8,2,3]{2,1,0:T(2,128)}), s32[8,2,3]{2,1,0:T(2,128)S(1)}, u32[]{:S(2)}, u32[]{:S(2)}) async-start(s32[8,2,3]{2,1,0:T(2,128)} %broadcast_in_dim.2), calls=%async_computation | async-start | bytes 16384 | tf_op jit(solution)/shard_map/all_to_all | solution.py:367
  8.7 0.9 %slice_bitcast_fusion = (bf16[4,64,64]{2,1,0:T(8,128)(2,1)S(1)}, bf16[4,64,64]{2,1,0:T(8,128)(2,1)S(1)}) fusion(bf16[32,1,64,64]{3,2,0,1:T(8,128)(2,1)} %bitcast.10), kind=kLoop, calls=%fused_computation | loop fusion | bytes 131072 | tf_op jit(solution)/shard_map/slice | solution.py:371
  9.5 4.8 %collective-permute-start.1 = (bf16[4,64,64]{2,1,0:T(8,128)(2,1)S(1)}, bf16[4,64,64]{2,1,0:T(8,128)(2,1)S(1)}, u32[]{:S(2)}, u32[]{:S(2)}) collective-permute-start(bf16[4,64,64]{2,1,0:T(8,128)(2,1)S(1)} %get-tuple-element.17), channel_id=1, source_target_pairs={{0,248},{8,0},{16,8},{24,16},{32,24},{40,32},{48,40},{56,48},{64,5... | collective-permute-start | bytes 98312 | tf_op jit(solution)/shard_map/ppermute | solution.py:355
  14.4 0.0 collective-permute-start
  14.4 0.5 all-to-all-done
  14.9 0.6 and_select_fusion.rows_ref.rows
  15.5 0.8 %collective-permute-done.1.after_ref = bf16[4,64,64]{2,1,0:T(8,128)(2,1)S(1)} collective-permute-done((bf16[4,64,64]{2,1,0:T(8,128)(2,1)S(1)}, bf16[4,64,64]{2,1,0:T(8,128)(2,1)S(1)}, u32[]{:S(2)}, u32[]{:S(2)}) %collective-permute-start.1) | collective-permute-done | bytes 32800 | tf_op jit(solution)/shard_map/ppermute | solution.py:355
  16.3 3.9 %collective-permute-done.before_ref = bf16[4,64,64]{2,1,0:T(8,128)(2,1)S(1)} collective-permute-done((bf16[4,64,64]{2,1,0:T(8,128)(2,1)S(1)}, bf16[4,64,64]{2,1,0:T(8,128)(2,1)S(1)}, u32[]{:S(2)}, u32[]{:S(2)}) %collective-permute-start) | collective-permute-done | bytes 32800 | tf_op jit(solution)/shard_map/ppermute | solution.py:355
  20.2 2.0 %pack.1 = bf16[8,3,64,128]{3,2,1,0:T(8,128)(2,1)} custom-call(s32[8,2,3]{2,1,0:T(2,128)} %and_select_fusion.rows_ref.rows, bf16[32,64,64]{2,1,0:T(8,128)(2,1)} %bitcast.11, bf16[4,64,64]{2,1,0:T(8,128)(2,1)S(1)} %collective-permute-done.before_ref, bf16[4,64,64]{2,1,0:T(8,128)(2,1)S(1)} %collective-permute-done.1.after_ref), custom_call_target="tpu_custom_call" | custom-call | bytes 1048576 | tf_op jit(solution)/shard_map/pack/pallas_call | solution.py:146
  22.2 7.8 %all-to-all-start.1 = ((bf16[8,3,64,128]{3,2,1,0:T(8,128)(2,1)}), bf16[8,3,64,128]{3,2,1,0:T(8,128)(2,1)S(1)}, u32[]{:S(2)}, u32[]{:S(2)}) async-start(bf16[8,3,64,128]{3,2,1,0:T(8,128)(2,1)} %pack.1), calls=%async_computation.1 | async-start | bytes 786432 | tf_op jit(solution)/shard_map/all_to_all | solution.py:374
  30.0 9.7 %fit.1 = (bf16[2,64,96,384]{3,2,1,0:T(8,128)(2,1)}, s32[18]{0:T(128)}) custom-call(s32[2,3]{1,0:T(2,128)} %names.1, s32[8,1024]{1,0:T(8,128)} %bitcast.12, bf16[2,64,64]{2,1,0:T(8,128)(2,1)} %metric_ref.1, bf16[2,64,36864]{2,1,0:T(8,128)(2,1)} %raw_ref.1), custom_call_target="tpu_custom_call" | custom-call | flops 603979776 | bytes 18874368 | tf_op jit(solution)/shard_map/fit/pallas_call | solution.py:99
  39.7 0.0 all-to-all-done.1.recv_ref
  39.8 10.4 %mix.1 = bf16[8,3,64,128]{3,2,1,0:T(8,128)(2,1)} custom-call(s32[18]{0:T(128)} %get-tuple-element.11.slots_ref, bf16[2,64,96,384]{3,2,1,0:T(8,128)(2,1)} %get-tuple-element.12.fit_ref, bf16[8,3,64,128]{3,2,1,0:T(8,128)(2,1)S(1)} %all-to-all-done.1.recv_ref), custom_call_target="tpu_custom_call" | custom-call | flops 3623878656 | bytes 9437184 | tf_op jit(solution)/shard_map/mix/pallas_call | solution.py:228
  50.2 15.6 %all_to_all.15.terms_ref = bf16[8,3,64,128]{3,2,1,0:T(8,128)(2,1)S(1)} all-to-all(bf16[8,3,64,128]{3,2,1,0:T(8,128)(2,1)} %mix.1), channel_id=1, replica_groups=mesh['ta'=32,'dev'=8] {'dev'}, dimensions={0} | all-to-all | bytes 786432 | tf_op jit(solution)/shard_map/all_to_all | solution.py:377
  65.8 1.9 %halo_sums.1 = (f32[2,64,128]{2,1,0:T(8,128)}, f32[2,64,128]{2,1,0:T(8,128)}) custom-call(s32[8,2,3]{2,1,0:T(2,128)} %and_select_fusion.rows_ref.rows, bf16[8,3,64,128]{3,2,1,0:T(8,128)(2,1)S(1)} %all_to_all.15.terms_ref), custom_call_target="tpu_custom_call" | custom-call | bytes 524288 | tf_op jit(solution)/shard_map/halo_sums/pallas_call | solution.py:281
  67.7 0.0 collective-permute-start.2
  67.7 3.9 %collective-permute-start.3 = (f32[2,64,128]{2,1,0:T(8,128)}, f32[2,64,128]{2,1,0:T(8,128)S(1)}, u32[]{:S(2)}, u32[]{:S(2)}) collective-permute-start(f32[2,64,128]{2,1,0:T(8,128)} %get-tuple-element.16), channel_id=1, source_target_pairs={{0,248},{8,0},{16,8},{24,16},{32,24},{40,32},{48,40},{56,48},{64,5... | collective-permute-start | bytes 196616 | tf_op jit(solution)/shard_map/ppermute | solution.py:355
  71.6 2.5 %own_sums.1 = (f32[32,64,64]{2,1,0:T(8,128)}, f32[8,64,64]{2,1,0:T(8,128)}) custom-call(s32[8,2,3]{2,1,0:T(2,128)} %and_select_fusion.rows_ref.rows, bf16[8,3,64,128]{3,2,1,0:T(8,128)(2,1)S(1)} %all_to_all.15.terms_ref), custom_call_target="tpu_custom_call" | custom-call | bytes 2097152 | tf_op jit(solution)/shard_map/own_sums/pallas_call | solution.py:309
  74.0 0.0 collective-permute-done.2.before_ref
  74.1 0.0 collective-permute-done.3.after_ref
  74.1 0.0 copy-start
  74.1 0.9 %copy-done = f32[8,64,64]{2,1,0:T(8,128)S(1)} copy-done((f32[8,64,64]{2,1,0:T(8,128)S(1)}, f32[8,64,64]{2,1,0:T(8,128)}, u32[]{:S(2)}) %copy-start) | copy-done | bytes 131096
  75.0 0.8 %add_edges.1 = f32[32,64,64]{2,1,0:T(8,128)} custom-call(f32[32,64,64]{2,1,0:T(8,128)} %get-tuple-element.13.own_ref, f32[8,64,64]{2,1,0:T(8,128)S(1)} %copy-done, f32[2,64,128]{2,1,0:T(8,128)S(1)} %collective-permute-done.2.before_ref, f32[2,64,128]{2,1,0:T(8,128)S(1)} %collective-permute-done.3.after_ref), custom_call_target="tpu_custom_call", output_to_operand_aliasing={{}: (0, {})} | custom-call | tf_op jit(solution)/shard_map/add_edges/pallas_call | solution.py:341
Async XLA Ops:
  1.3 13.6 %all-to-all-start = ((s32[8,2,3]{2,1,0:T(2,128)}), s32[8,2,3]{2,1,0:T(2,128)S(1)}, u32[]{:S(2)}, u32[]{:S(2)}) async-start(s32[8,2,3]{2,1,0:T(2,128)} %broadcast_in_dim.2), calls=%async_computation | async-start | bytes 16384 | tf_op jit(solution)/shard_map/all_to_all | solution.py:367
  9.5 6.7 %collective-permute-start.1 = (bf16[4,64,64]{2,1,0:T(8,128)(2,1)S(1)}, bf16[4,64,64]{2,1,0:T(8,128)(2,1)S(1)}, u32[]{:S(2)}, u32[]{:S(2)}) collective-permute-start(bf16[4,64,64]{2,1,0:T(8,128)(2,1)S(1)} %get-tuple-element.17), channel_id=1, source_target_pairs={{0,248},{8,0},{16,8},{24,16},{32,24},{40,32},{48,40},{56,48},{64,5... | collective-permute-start | bytes 98312 | tf_op jit(solution)/shard_map/ppermute | solution.py:355
  14.4 5.8 %collective-permute-start = (bf16[4,64,64]{2,1,0:T(8,128)(2,1)S(1)}, bf16[4,64,64]{2,1,0:T(8,128)(2,1)S(1)}, u32[]{:S(2)}, u32[]{:S(2)}) collective-permute-start(bf16[4,64,64]{2,1,0:T(8,128)(2,1)S(1)} %get-tuple-element.18), channel_id=1, source_target_pairs={{0,8},{8,16},{16,24},{24,32},{32,40},{40,48},{48,56},{56,64},{64,7... | collective-permute-start | bytes 98312 | tf_op jit(solution)/shard_map/ppermute | solution.py:355
  22.2 17.6 %all-to-all-start.1 = ((bf16[8,3,64,128]{3,2,1,0:T(8,128)(2,1)}), bf16[8,3,64,128]{3,2,1,0:T(8,128)(2,1)S(1)}, u32[]{:S(2)}, u32[]{:S(2)}) async-start(bf16[8,3,64,128]{3,2,1,0:T(8,128)(2,1)} %pack.1), calls=%async_computation.1 | async-start | bytes 786432 | tf_op jit(solution)/shard_map/all_to_all | solution.py:374
  67.7 6.3 %collective-permute-start.2 = (f32[2,64,128]{2,1,0:T(8,128)}, f32[2,64,128]{2,1,0:T(8,128)S(1)}, u32[]{:S(2)}, u32[]{:S(2)}) collective-permute-start(f32[2,64,128]{2,1,0:T(8,128)} %get-tuple-element.15), channel_id=1, source_target_pairs={{0,8},{8,16},{16,24},{24,32},{32,40},{40,48},{48,56},{56,64},{64,7... | collective-permute-start | bytes 196616 | tf_op jit(solution)/shard_map/ppermute | solution.py:355
  67.7 6.3 %collective-permute-start.3 = (f32[2,64,128]{2,1,0:T(8,128)}, f32[2,64,128]{2,1,0:T(8,128)S(1)}, u32[]{:S(2)}, u32[]{:S(2)}) collective-permute-start(f32[2,64,128]{2,1,0:T(8,128)} %get-tuple-element.16), channel_id=1, source_target_pairs={{0,248},{8,0},{16,8},{24,16},{32,24},{40,32},{48,40},{56,48},{64,5... | collective-permute-start | bytes 196616 | tf_op jit(solution)/shard_map/ppermute | solution.py:355
  74.1 1.0 %copy-start = (f32[8,64,64]{2,1,0:T(8,128)S(1)}, f32[8,64,64]{2,1,0:T(8,128)}, u32[]{:S(2)}) copy-start(f32[8,64,64]{2,1,0:T(8,128)} %get-tuple-element.14.edge_ref) | copy-start | bytes 393220
